TPU v7x, 32 devices: a whole 2x2x4 slice. The times are simulated.
32 devices in a mesh: seg: 8 (over y, x, core), head: 4 (over z).
Axes of the slice: x: 2, y: 2, z: 4, core: 2. Of those that a mesh axis runs over, the one named last changes fastest.
Arguments:
- tokens: float32 [4096, 2048], P(('seg', 'head'))
- document_index: int32 [4096], P('seg'), may hold values from 0 to 31, never falling along the last dimension, each value on 1 to 256 neighbouring positions
- block_mask: int32 [8, 4, 4], P('seg'), may hold values from 0 to 1, as said below
- slot_keys: bfloat16 [2, 128, 2048], P(None, None, 'head'), may hold values from -8 to 8
- mem_init: float32 [2, 128, 2048], P(None, None, 'head'), may hold values from -6 to 6
- retain: float32 [2, 8, 32], P(None, 'seg', 'head'), may hold values from 0.005 to 1
- attn_gain: float32 [2, 2048], replicated, may hold values from 0.25 to 4
- mlp_gain: float32 [2, 2048], replicated, may hold values from 0.25 to 4
- w_query: bfloat16 [2, 2048, 2048], P(None, None, 'head')
- w_kv: bfloat16 [2, 2048, 1024], P(None, None, 'head')
- w_out: bfloat16 [2, 2048, 2048], P(None, 'head'), may hold values from -0.125 to 0.125
- w_gate_up: bfloat16 [2, 2048, 2, 4096], P(None, None, None, 'head'), may hold values from -0.125 to 0.125
- w_down: bfloat16 [2, 4096, 2048], P(None, 'head'), may hold values from -0.09375 to 0.09375
Outputs:
- hidden: float32 [4096, 2048], P(('seg', 'head'))
- memory: float32 [2, 8, 128, 2048], P(None, 'seg', None, 'head')
Inputs may be any that keep to these rules, and one draw needn't show every extreme that they name: `document_index`: document numbers never fall along the sequence. `block_mask`: in every segment the blocks on the diagonal are 1 and the blocks above it 0.
All inputs are finite; a program needn't handle non-finite values.
Results may differ from a plain program's by a relative error of at most 0.025.
Values may be sent and summed in bfloat16 or wider, within the bound.
A program may use at most 192 MiB of HBM per device.

v0:
```python
import jax
import jax.numpy as jnp
from jax import lax
from jax.sharding import PartitionSpec as P

HEADS = 32
KV_HEADS = 8
HD = 64
MEM = 128
SEG_LEN = 512
BLOCK = 128
DEPTH_NUMBER = 2


def prefix(x, axis, combine, identity):
    count, here = (lax.axis_size(axis), lax.axis_index(axis))
    everything = jax.tree.map(lambda part: lax.all_gather(part, axis), x)
    start = jax.tree.map(
        lambda part, zero: jnp.broadcast_to(jnp.asarray(zero, part.dtype), part.shape), x, identity
    )

    def hop(k, before):
        reached = k < here
        new = combine(before, jax.tree.map(lambda part: part[k], everything))
        return jax.tree.map(lambda a, b: jnp.where(reached, a, b), new, before)

    return lax.fori_loop(0, count, hop, start)


def rms_norm(value, gain):
    factor = lax.rsqrt(jnp.mean(value * value, axis=-1, keepdims=True) + 1e-05)
    return (value * factor * gain).astype(jnp.bfloat16)


def rope_tables(position):
    half = HD // 2
    freq = 500000.0 ** (-(jnp.arange(half).astype(jnp.float32) * 2.0 / HD))
    angle = position.astype(jnp.float32)[:, None] * freq[None, :]
    return (jnp.cos(angle), jnp.sin(angle))


def rotate(tensor, cosine, sine):
    half = tensor.shape[-1] // 2
    first = tensor[..., :half]
    second = tensor[..., half:]
    cos_part = cosine[:, None, :]
    sin_part = sine[:, None, :]
    return jnp.concatenate(
        [first * cos_part - second * sin_part, second * cos_part + first * sin_part], axis=-1
    )


def combine(earlier, later):
    return (earlier[0] * later[0], later[0] * earlier[1] + later[1])


def body(
    tokens,
    document_index,
    block_mask,
    slot_keys,
    mem_init,
    retain,
    attn_gain,
    mlp_gain,
    w_query,
    w_kv,
    w_out,
    w_gate_up,
    w_down,
):
    seg_local = document_index.shape[0] // SEG_LEN
    rows_all = seg_local * SEG_LEN
    cols_query = w_query.shape[2]
    local_heads = cols_query // HD
    group = HEADS // KV_HEADS
    local_kv = local_heads // group
    scale = HD ** (-0.5)
    cosine, sine = rope_tables(jnp.arange(rows_all) % SEG_LEN)
    docs = document_index.reshape(seg_local, SEG_LEN)
    causal = jnp.arange(SEG_LEN)[:, None] >= jnp.arange(SEG_LEN)[None, :]
    stream = tokens
    stored = []
    for layer in range(DEPTH_NUMBER):
        query_weight = w_query[layer]
        pair_weight = w_kv[layer]
        out_weight = w_out[layer]
        widening_matrix = w_gate_up[layer]
        down_weight = w_down[layer]
        normed = rms_norm(stream, attn_gain[layer])
        project_piece = lax.all_gather(normed, "head", axis=0, tiled=True)
        projected = jnp.concatenate(
            [
                jnp.dot(project_piece, query_weight, preferred_element_type=jnp.float32),
                jnp.dot(project_piece, pair_weight, preferred_element_type=jnp.float32),
            ],
            axis=1,
        )
        query = rotate(
            projected[:, :cols_query].reshape(rows_all, local_heads, HD), cosine, sine
        ).astype(jnp.bfloat16)
        pairs = projected[:, cols_query:].reshape(rows_all, local_kv, 2, HD)
        lookup_vectors = rotate(pairs[:, :, 0], cosine, sine).astype(jnp.bfloat16)
        values = pairs[:, :, 1].astype(jnp.bfloat16)
        query = query.reshape(seg_local, SEG_LEN, local_kv, group, HD)
        lookup_vectors = lookup_vectors.reshape(seg_local, SEG_LEN, local_kv, HD)
        values = values.reshape(seg_local, SEG_LEN, local_kv, HD)
        slots = slot_keys[layer].reshape(MEM, local_kv, group, HD)
        write_scores = (
            jnp.einsum(
                "mkgd,sjkd->skgmj", slots, lookup_vectors, preferred_element_type=jnp.float32
            )
            * scale
        )
        write_probs = jax.nn.softmax(write_scores, axis=-1).astype(jnp.bfloat16)
        written = jnp.einsum(
            "skgmj,sjkd->smkgd", write_probs, values, preferred_element_type=jnp.float32
        ).reshape(seg_local, MEM, cols_query)
        rates = jnp.repeat(retain[layer], HD, axis=1)[:, None, :]
        keep_total = jnp.ones((1, cols_query), jnp.float32)
        add_total = jnp.zeros((MEM, cols_query), jnp.float32)
        segment = 0
        keep_total = keep_total * rates[segment]
        add_total = rates[segment] * add_total + (1.0 - rates[segment]) * written[segment]
        identity = (
            jnp.ones((1, cols_query), jnp.float32),
            jnp.zeros((MEM, cols_query), jnp.float32),
        )
        keep_before, add_before = prefix((keep_total, add_total), "seg", combine, identity)
        state = keep_before * mem_init[layer] + add_before
        segment = 0
        memory_read = state.astype(jnp.bfloat16).reshape(MEM, local_kv, group, HD)
        state = rates[segment] * state + (1.0 - rates[segment]) * written[segment]
        after_list = [state]
        blocks = jnp.repeat(jnp.repeat(block_mask[segment], BLOCK, axis=0), BLOCK, axis=1)
        allowed = causal & (docs[segment][:, None] == docs[segment][None, :]) & (blocks == 1)
        slot_scores = (
            jnp.einsum("ikgd,mkgd->kgim", query[segment], slots, preferred_element_type=jnp.float32)
            * scale
        )
        token_scores = (
            jnp.einsum(
                "ikgd,jkd->kgij",
                query[segment],
                lookup_vectors[segment],
                preferred_element_type=jnp.float32,
            )
            * scale
        )
        token_scores = jnp.where(allowed, token_scores, -jnp.inf)
        probs = jax.nn.softmax(
            jnp.concatenate([slot_scores, token_scores], axis=-1), axis=-1
        ).astype(jnp.bfloat16)
        result = jnp.einsum(
            "kgim,mkgd->ikgd", probs[..., :MEM], memory_read, preferred_element_type=jnp.float32
        )
        result = result + jnp.einsum(
            "kgij,jkd->ikgd", probs[..., MEM:], values[segment], preferred_element_type=jnp.float32
        )
        outputs = result.reshape(SEG_LEN, cols_query).astype(jnp.bfloat16)
        stored.append(jnp.stack(after_list))
        mixed = lax.psum_scatter(
            jnp.dot(outputs, out_weight, preferred_element_type=jnp.float32),
            "head",
            scatter_dimension=0,
            tiled=True,
        )
        middle = stream + mixed
        both = jnp.einsum(
            "rd,dtf->rtf",
            lax.all_gather(rms_norm(middle, mlp_gain[layer]), "head", axis=0, tiled=True),
            widening_matrix,
            preferred_element_type=jnp.float32,
        )
        inner = (jax.nn.silu(both[:, 0]) * both[:, 1]).astype(jnp.bfloat16)
        down = lax.psum_scatter(
            jnp.dot(inner, down_weight, preferred_element_type=jnp.float32),
            "head",
            scatter_dimension=0,
            tiled=True,
        )
        stream = middle + down
    return (stream, jnp.stack(stored))


def solution(mesh):
    return jax.shard_map(
        body,
        mesh=mesh,
        in_specs=(
            P(("seg", "head"), None),
            P("seg"),
            P("seg", None, None),
            P(None, None, "head"),
            P(None, None, "head"),
            P(None, "seg", "head"),
            P(),
            P(),
            P(None, None, "head"),
            P(None, None, "head"),
            P(None, "head", None),
            P(None, None, None, "head"),
            P(None, "head", None),
        ),
        out_specs=(P(("seg", "head"), None), P(None, "seg", None, "head")),
        check_vma=False,
    )
```

profile of v0, /device:TPU:16, one launch (start us, length us, event | category | flops | bytes accessed | tf_op | source)
XLA Modules:
  0.0 654.3 jit_solution(11971218342031773427)
XLA Ops:
  16.0 4.5 slice_bitcast_fusion
  20.5 37.0 %all-gather.7.cloned.1.call-done = bf16[512,2048]{1,0:T(8,128)(2,1)} async-done(((bf16[128,2048]{1,0:T(8,128)(2,1)}), bf16[512,2048]{1,0:T(8,128)(2,1)}) %all-gather.7.cloned.1.call-update) | async-done | bytes 2097168 | tf_op jit(solution)/shard_map/all_gather | solution.py:91
  62.6 4.0 copy.66
  66.8 9.0 %all_gather.26 = f32[8,1,512]{2,1,0:T(1,128)S(1)} all-gather(f32[1,1,512]{2,1,0:T(1,128)S(1)} %broadcast_in_dim.27), channel_id=1, replica_groups=mesh['seg'=8,'head'=4] {'seg'}, dimensions={0}, use_global_device_ids=true | all-gather | bytes 18432 | tf_op jit(solution)/shard_map/all_gather | solution.py:17
  83.0 4.6 divide_convert_fusion.1
  90.8 9.6 %while.32 = (s32[]{:T(128)}, f32[1,512]{1,0:T(1,128)S(1)}, f32[128,512]{1,0:T(8,128)S(1)}, s32[]{:T(128)}, f32[8,1,512]{2,1,0:T(1,128)S(1)}, /*index=5*/f32[8,128,512]{2,1,0:T(8,128)}, s32[]{:T(128)}, s32[]{:T(128)}) while((s32[]{:T(128)}, f32[1,512]{1,0:T(1,128)S(1)}, f32[128,512]{1,0:T(8,128)S(1)}, s32[]{:T(128)}, ...), condition=%wide.region_4.5_spmd.clone, body=%wide.region_3.4_spmd.clone.sunk | while | flops 263684 | bytes 796787 | solution.py:27
  103.1 4.8 fusion.31
  109.2 75.7 %reduce-scatter.5.cloned.1.call-done = f32[128,2048]{1,0:T(8,128)} async-done(((f32[512,2048]{1,0:T(8,128)}), f32[128,2048]{1,0:T(8,128)}) %reduce-scatter.5.cloned.1.call-update) | async-done | bytes 1048592 | tf_op jit(solution)/shard_map/reduce_scatter | solution.py:162
  187.6 14.1 %fusion.92 = (bf16[1,2048,2,1024]{3,2,1,0:T(2,128)(2,1)}, bf16[1,2048,2,1024]{3,2,1,0:T(2,128)(2,1)}) fusion(bf16[2,2048,2,1024]{3,2,1,0:T(2,128)(2,1)} %param.28), kind=kLoop, calls=%fused_computation.164 | loop fusion | bytes 33554432 | tf_op jit(solution)/shard_map/slice | solution.py:88
  201.7 30.3 %all-gather.11.cloned.1.call-done = bf16[512,2048]{1,0:T(8,128)(2,1)} async-done(((bf16[128,2048]{1,0:T(8,128)(2,1)}), bf16[512,2048]{1,0:T(8,128)(2,1)}) %all-gather.11.cloned.1.call-update) | async-done | bytes 2097168 | tf_op jit(solution)/shard_map/all_gather | solution.py:171
  232.1 8.3 %fusion.5 = f32[512,2,1024]{2,0,1:T(8,128)S(1)} fusion(bf16[1,2048,2,1024]{3,2,1,0:T(2,128)(2,1)} %get-tuple-element.307, bf16[512,2048]{1,0:T(8,128)(2,1)} %all-gather.11.cloned.1.call-done), kind=kOutput, calls=%fused_computation.19 | convolution fusion | flops 4294967296 | bytes 14680064 | tf_op jit(solution)/shard_map/rd,dtf->rtf/dot_general | solution.py:169
  240.4 6.6 %fusion.14 = f32[512,2048]{1,0:T(8,128)} fusion(bf16[2,1024,2048]{2,1,0:T(8,128)(2,1)} %param.29, f32[512,2,1024]{2,0,1:T(8,128)S(1)} %fusion.5), kind=kOutput, calls=%fused_computation.30 | convolution fusion | flops 2150629376 | bytes 12582912 | tf_op jit(solution)/shard_map/dot_general | solution.py:177
  247.1 77.6 %reduce-scatter.7.cloned.1.call-done = f32[128,2048]{1,0:T(8,128)} async-done(((f32[512,2048]{1,0:T(8,128)}), f32[128,2048]{1,0:T(8,128)}) %reduce-scatter.7.cloned.1.call-update) | async-done | bytes 1048592 | tf_op jit(solution)/shard_map/reduce_scatter | solution.py:176
  328.1 43.7 %all-gather.13.cloned.1.call-done = bf16[512,2048]{1,0:T(8,128)(2,1)} async-done(((bf16[128,2048]{1,0:T(8,128)(2,1)}), bf16[512,2048]{1,0:T(8,128)(2,1)}) %all-gather.13.cloned.1.call-update) | async-done | bytes 2097168 | tf_op jit(solution)/shard_map/all_gather | solution.py:91
  377.8 4.0 copy.78
  381.8 10.0 %all_gather.30 = f32[8,1,512]{2,1,0:T(1,128)} all-gather(f32[1,1,512]{2,1,0:T(1,128)S(1)} %broadcast_in_dim.64), channel_id=1, replica_groups=mesh['seg'=8,'head'=4] {'seg'}, dimensions={0}, use_global_device_ids=true | all-gather | bytes 18432 | tf_op jit(solution)/shard_map/all_gather | solution.py:17
  399.2 4.7 divide_convert_fusion
  407.1 14.9 %while.33 = (s32[]{:T(128)}, f32[1,512]{1,0:T(1,128)S(1)}, f32[128,512]{1,0:T(8,128)S(1)}, s32[]{:T(128)}, f32[8,1,512]{2,1,0:T(1,128)}, /*index=5*/f32[8,128,512]{2,1,0:T(8,128)}, s32[]{:T(128)}, s32[]{:T(128)}) while((s32[]{:T(128)}, f32[1,512]{1,0:T(1,128)S(1)}, f32[128,512]{1,0:T(8,128)S(1)}, s32[]{:T(128)}, ...), condition=%wide.region_15.16_spmd.clone, body=%wide.region_14.15_spmd.clone.sunk | while | flops 263684 | bytes 796787 | solution.py:27
  424.0 4.9 fusion.25
  428.9 76.6 %reduce-scatter.9.cloned.1.call-done = f32[128,2048]{1,0:T(8,128)} async-done(((f32[512,2048]{1,0:T(8,128)}), f32[128,2048]{1,0:T(8,128)}) %reduce-scatter.9.cloned.1.call-update) | async-done | bytes 1048592 | tf_op jit(solution)/shard_map/reduce_scatter | solution.py:162
  508.3 44.4 %all-gather.17.cloned.1.call-done = bf16[512,2048]{1,0:T(8,128)(2,1)} async-done(((bf16[128,2048]{1,0:T(8,128)(2,1)}), bf16[512,2048]{1,0:T(8,128)(2,1)}) %all-gather.17.cloned.1.call-update) | async-done | bytes 2097168 | tf_op jit(solution)/shard_map/all_gather | solution.py:171
  552.7 8.3 %fusion.4 = f32[512,2,1024]{2,0,1:T(8,128)S(1)} fusion(bf16[1,2048,2,1024]{3,2,1,0:T(2,128)(2,1)} %get-tuple-element.306, bf16[512,2048]{1,0:T(8,128)(2,1)} %all-gather.17.cloned.1.call-done), kind=kOutput, calls=%fused_computation.17 | convolution fusion | flops 4294967296 | bytes 14680064 | tf_op jit(solution)/shard_map/rd,dtf->rtf/dot_general | solution.py:169
  561.0 6.6 %fusion.12 = f32[512,2048]{1,0:T(8,128)} fusion(bf16[2,1024,2048]{2,1,0:T(8,128)(2,1)} %param.29, f32[512,2,1024]{2,0,1:T(8,128)S(1)} %fusion.4), kind=kOutput, calls=%fused_computation.28 | convolution fusion | flops 2150629376 | bytes 12582912 | tf_op jit(solution)/shard_map/dot_general | solution.py:177
  569.6 75.5 %reduce-scatter.11.cloned.1.call-done = f32[128,2048]{1,0:T(8,128)} async-done(((f32[512,2048]{1,0:T(8,128)}), f32[128,2048]{1,0:T(8,128)}) %reduce-scatter.11.cloned.1.call-update) | async-done | bytes 1048592 | tf_op jit(solution)/shard_map/reduce_scatter | solution.py:176
  (193 shorter events, 83.8 us)
Async XLA Ops:
  7.2 4.6 copy-start.4
  7.2 50.3 %all-gather.7.cloned.1.call-start = ((), (), s32[]{:S(2)}) async-start(), calls=%async_computation.4 | async-start | bytes 2621440 | tf_op jit(solution)/shard_map/all_gather | solution.py:91
  11.7 79.1 %all-gather.9.cloned.1.call-start = ((), (), s32[]{:S(2)}) async-start(), calls=%async_computation.5 | async-start | bytes 2359296 | tf_op jit(solution)/shard_map/all_gather | solution.py:17
  12.9 2.4 copy-start.10
  62.3 122.7 %reduce-scatter.5.cloned.1.call-start = ((), (), s32[]{:S(2)}) async-start(), calls=%async_computation.6 | async-start | bytes 5242880 | tf_op jit(solution)/shard_map/reduce_scatter | solution.py:162
  62.6 4.0 copy-start.25
  66.8 13.2 %copy-start.15 = (pred[512,512]{0,1:T(8,128)(4,1)}, pred[512,512]{0,1:T(8,128)(4,1)S(1)}, u32[]{:S(2)}) copy-start(pred[512,512]{0,1:T(8,128)(4,1)S(1)} %fusion.63) | copy-start | bytes 786436
  107.9 77.0 %copy-start.2 = (f32[128,2048]{1,0:T(8,128)S(1)}, f32[128,2048]{1,0:T(8,128)}, u32[]{:S(2)}) copy-start(f32[128,2048]{1,0:T(8,128)} %param.17) | copy-start | bytes 3145732
  107.9 124.1 %all-gather.11.cloned.1.call-start = ((), (), s32[]{:S(2)}) async-start(), calls=%async_computation.7 | async-start | bytes 2621440 | tf_op jit(solution)/shard_map/all_gather | solution.py:171
  187.3 137.3 %reduce-scatter.7.cloned.1.call-start = ((), (), s32[]{:S(2)}) async-start(), calls=%async_computation.8 | async-start | bytes 5242880 | tf_op jit(solution)/shard_map/reduce_scatter | solution.py:176
  247.0 80.1 %copy-start.3 = (bf16[256,2048]{0,1:T(8,128)(2,1)S(1)}, bf16[256,2048]{0,1:T(8,128)(2,1)}, u32[]{:S(2)}) copy-start(bf16[256,2048]{0,1:T(8,128)(2,1)} %get-tuple-element.310) | copy-start | bytes 3145732
  247.0 124.8 %all-gather.13.cloned.1.call-start = ((), (), s32[]{:S(2)}) async-start(), calls=%async_computation.9 | async-start | bytes 2621440 | tf_op jit(solution)/shard_map/all_gather | solution.py:91
  327.1 80.0 %all-gather.15.cloned.1.call-start = ((), (), s32[]{:S(2)}) async-start(), calls=%async_computation.10 | async-start | bytes 2359296 | tf_op jit(solution)/shard_map/all_gather | solution.py:17
  328.1 46.1 %copy-start.22 = (f32[512]{0:T(512)}, f32[512]{0:T(512)S(1)}, u32[]{:S(2)}) copy-start(f32[512]{0:T(512)S(1)} %broadcast_in_dim.65) | copy-start | bytes 6148
  328.1 48.0 %copy-start.20 = (f32[512]{0:T(512)}, f32[512]{0:T(512)S(1)}, u32[]{:S(2)}) copy-start(f32[512]{0:T(512)S(1)} %get-tuple-element.335) | copy-start | bytes 6148
  375.9 5.9 copy-start.6
  376.8 128.7 %reduce-scatter.9.cloned.1.call-start = ((), (), s32[]{:S(2)}) async-start(), calls=%async_computation.11 | async-start | bytes 5242880 | tf_op jit(solution)/shard_map/reduce_scatter | solution.py:162
  407.0 15.1 %copy-start.7 = (f32[2,64,4,128]{3,1,2,0:T(8,128)S(1)}, f32[2,64,4,128]{3,1,2,0:T(8,128)}, u32[]{:S(2)}) copy-start(f32[2,64,4,128]{3,1,2,0:T(8,128)} %copy-done.6) | copy-start | bytes 786436
  407.1 15.1 %copy-start.8 = (f32[1,128,512]{1,2,0:T(8,128)S(1)}, f32[1,128,512]{1,2,0:T(8,128)}, u32[]{:S(2)}) copy-start(f32[1,128,512]{1,2,0:T(8,128)} %copy.98) | copy-start | bytes 786436
  407.1 15.1 %copy-start.21 = (f32[512]{0:T(512)S(1)}, f32[512]{0:T(512)}, u32[]{:S(2)}) copy-start(f32[512]{0:T(512)} %copy-done.20) | copy-start | bytes 6148
  407.1 15.1 %copy-start.23 = (f32[512]{0:T(512)S(1)}, f32[512]{0:T(512)}, u32[]{:S(2)}) copy-start(f32[512]{0:T(512)} %copy-done.22) | copy-start | bytes 6148
  428.9 78.1 %copy-start.19 = (f32[1,2048]{1,0:T(1,128)S(1)}, f32[1,2048]{1,0:T(1,128)}, u32[]{:S(2)}) copy-start(f32[1,2048]{1,0:T(1,128)} %get-tuple-element.328) | copy-start | bytes 24580
  428.9 123.8 %all-gather.17.cloned.1.call-start = ((), (), s32[]{:S(2)}) async-start(), calls=%async_computation.12 | async-start | bytes 2621440 | tf_op jit(solution)/shard_map/all_gather | solution.py:171
  508.0 137.1 %reduce-scatter.11.cloned.1.call-start = ((), (), s32[]{:S(2)}) async-start(), calls=%async_computation.13 | async-start | bytes 5242880 | tf_op jit(solution)/shard_map/reduce_scatter | solution.py:176
  (14 other events, 17.5 us)
Sparse Core Ops, SparseCore 0:
  11.8 45.6 all-gather.6
  62.4 27.9 all-gather.8
  108.1 76.8 reduce-scatter.4
  187.5 44.5 all-gather.10
  247.1 77.4 reduce-scatter.6
  327.2 44.5 all-gather.12
  376.9 28.0 all-gather.14
  429.0 76.5 reduce-scatter.8
  508.1 44.5 all-gather.16
  567.7 77.3 reduce-scatter.10
where the time goes:
time: 657 us; the launch traced here: 654 us
  waiting for transfers between devices  461 us (70%)
  matrix products  66.4 us (10%)
  other arithmetic  53.8 us (8%)
  local copies, waits for them, and re-layouts  37.8 us (6%)
  blocking collectives  19.1 us (3%)
  between operations  14.8 us (2%)
    reduce_scatter x2, waiting for transfers between devices, body(): lax.psum_scatter(jnp.dot(inner, down_weight, preferred_element_type=jnp.f...  153 us
    reduce_scatter x2, waiting for transfers between devices, body(): lax.psum_scatter(jnp.dot(outputs, out_weight, preferred_element_type=jnp....  152 us
    all_gather x2, waiting for transfers between devices, body(): project_piece = lax.all_gather(normed, 'head', axis=0, tiled=True)  80.7 us
    all_gather x2, waiting for transfers between devices, body(): lax.all_gather(rms_norm(middle, mlp_gain[layer]), 'head', axis=0, tiled=T...  74.7 us
    select_n x32, other arithmetic, hop(): return jax.tree.map(lambda a, b: jnp.where(reached, a, b), new, before)  24.1 us
    all_gather x2, blocking collectives, prefix(): everything = jax.tree.map(lambda part: lax.all_gather(part, axis), x)  19.1 us
    dot_general x2, matrix products, body(): jnp.einsum('rd,dtf->rtf', lax.all_gather(rms_norm(middle, mlp_gain[layer]...  16.6 us
    slice x1, local copies, waits for them, and re-layouts, body(): widening_matrix = w_gate_up[layer]  14.1 us
  transfers between devices with their start and end apart: 10, of which 8 were waited for; matrix products, arithmetic and copies ran while one was open for 10% of the time, Pallas kernels for 0%

commit v1 on v0

--- a/solution.py
+++ b/solution.py
@@ -1,6 +1,11 @@
+import functools
+
 import jax
 import jax.numpy as jnp
+import numpy as np
 from jax import lax
+from jax.experimental import pallas as pl
+from jax.experimental.pallas import tpu as pltpu
 from jax.sharding import PartitionSpec as P
 
 HEADS = 32
@@ -10,6 +15,501 @@
 SEG_LEN = 512
 BLOCK = 128
 DEPTH_NUMBER = 2
+CHUNK = 32
+LAG = 4
+MESH = pl.DeviceIdType.MESH
+F32 = jnp.float32
+BF16 = jnp.bfloat16
+
+
+def enter(me, n):
+    barrier = pltpu.get_barrier_semaphore()
+
+    @pl.when(me > 0)
+    def _():
+        pl.semaphore_signal(barrier, inc=1, device_id={"head": me - 1}, device_id_type=MESH)
+
+    @pl.when(me < n - 1)
+    def _():
+        pl.semaphore_signal(barrier, inc=1, device_id={"head": me + 1}, device_id_type=MESH)
+
+    @pl.when((me > 0) & (me < n - 1))
+    def _():
+        pl.semaphore_wait(barrier, 2)
+
+    @pl.when((me == 0) | (me == n - 1))
+    def _():
+        pl.semaphore_wait(barrier, 1)
+
+
+def remote(source, target, send, recv, to):
+    return pltpu.make_async_remote_copy(
+        src_ref=source,
+        dst_ref=target,
+        send_sem=send,
+        recv_sem=recv,
+        device_id={"head": to},
+        device_id_type=MESH,
+    )
+
+
+def normed_rows(value, gain):
+    factor = lax.rsqrt(jnp.mean(value * value, axis=-1, keepdims=True) + 1e-05)
+    return (value * factor * gain).astype(BF16)
+
+
+def rope_lanes(value, cosine, sine):
+    lane = lax.broadcasted_iota(jnp.int32, value.shape, 1)
+    turned = jnp.where(lane % HD < HD // 2, pltpu.roll(value, 96, 1), pltpu.roll(value, 32, 1))
+    return value * cosine + turned * sine
+
+
+def project_rows(rows, x, wq, wkv, tables, q_out, kv_out):
+    cosine, sine, cosine_kv, sine_kv = (table[rows, :] for table in tables)
+    block = x[rows, :]
+    query = jnp.dot(block, wq[...], preferred_element_type=F32)
+    for at in range(0, query.shape[1], 128):
+        q_out[rows, at : at + 128] = rope_lanes(query[:, at : at + 128], cosine, sine).astype(BF16)
+    pairs = jnp.dot(block, wkv[...], preferred_element_type=F32)
+    for at in range(0, pairs.shape[1], 128):
+        kv_out[rows, at : at + 128] = rope_lanes(
+            pairs[:, at : at + 128], cosine_kv, sine_kv
+        ).astype(BF16)
+
+
+def widen_rows(rows, x, w, out):
+    block = x[rows, :]
+    tile = 256
+
+    def step(i, carry):
+        cols = pl.ds(pl.multiple_of(i * tile, tile), tile)
+        gate = jnp.dot(block, w[0, :, cols], preferred_element_type=F32)
+        up = jnp.dot(block, w[1, :, cols], preferred_element_type=F32)
+        out[rows, cols] = (gate / (1.0 + jnp.exp(-gate)) * up).astype(BF16)
+        return carry
+
+    lax.fori_loop(0, out.shape[1] // tile, step, 0)
+
+
+def partial_rows(rows, x, w, part):
+    block = x[rows, :]
+    tile = 512
+
+    def step(i, carry):
+        cols = pl.ds(pl.multiple_of(i * tile, tile), tile)
+        part[rows, cols] = jnp.dot(block, w[:, cols], preferred_element_type=F32)
+        return carry
+
+    lax.fori_loop(0, part.shape[1] // tile, step, 0)
+
+
+def add_rest(me, n, part, rest):
+    held = rest.shape[0]
+    if held * n == part.shape[0]:
+        rows = pl.ds(pl.multiple_of(me * held, held), held)
+        part[rows, :] += rest[...]
+    else:
+
+        @pl.when(me == 0)
+        def _():
+            part[:held, :] += rest[...]
+
+        @pl.when(me == n - 1)
+        def _():
+            part[held:, :] += rest[...]
+
+
+def gather_kernel(n, layer, tokens, gain, wq_hbm, wkv_hbm, cos_q, sin_q, cos_kv, sin_kv,
+                  q_out, kv_out, x, wq, wkv, load, send, recv):
+    me = lax.axis_index("head")
+    loads = [
+        pltpu.make_async_copy(wq_hbm.at[layer], wq, load.at[0]),
+        pltpu.make_async_copy(wkv_hbm.at[layer], wkv, load.at[1]),
+    ]
+    for copy in loads:
+        copy.start()
+    mine = tokens.shape[0]
+    pieces = mine // CHUNK
+    enter(me, n)
+
+    def hop(way, shard, piece):
+        rows = pl.ds(pl.multiple_of(shard * mine + piece * CHUNK, CHUNK), CHUNK)
+        to = me + 1 if way == 0 else me - 1
+        to = jnp.clip(to, 0, n - 1)
+        at = shard * pieces + piece
+        return remote(x.at[rows], x.at[rows], send.at[way, at], recv.at[way, at], to)
+
+    for piece in range(pieces):
+        rows = pl.ds(pl.multiple_of(me * mine + piece * CHUNK, CHUNK), CHUNK)
+        x[rows, :] = normed_rows(tokens[piece * CHUNK : (piece + 1) * CHUNK, :], gain[...])
+
+        @pl.when(me < n - 1)
+        def _():
+            hop(0, me, piece).start()
+
+        @pl.when(me > 0)
+        def _():
+            hop(1, me, piece).start()
+
+    for copy in loads:
+        copy.wait()
+    tables = (cos_q, sin_q, cos_kv, sin_kv)
+
+    def project(shard):
+        rows = pl.ds(pl.multiple_of(shard * mine, mine), mine)
+        project_rows(rows, x, wq, wkv, tables, q_out, kv_out)
+
+    project(me)
+    for far in range(1, n):
+        for piece in range(pieces):
+
+            @pl.when(me - far >= 0)
+            def _():
+                hop(0, me - far, piece).wait_recv()
+
+                @pl.when(me < n - 1)
+                def _():
+                    hop(0, me - far, piece).start()
+
+            @pl.when(me + far < n)
+            def _():
+                hop(1, me + far, piece).wait_recv()
+
+                @pl.when(me > 0)
+                def _():
+                    hop(1, me + far, piece).start()
+
+        @pl.when(me - far >= 0)
+        def _():
+            project(me - far)
+
+        @pl.when(me + far < n)
+        def _():
+            project(me + far)
+
+    for shard in range(n):
+        for piece in range(pieces):
+
+            @pl.when((shard <= me) & (me < n - 1))
+            def _():
+                hop(0, shard, piece).wait_send()
+
+            @pl.when((shard >= me) & (me > 0))
+            def _():
+                hop(1, shard, piece).wait_send()
+
+
+def exchange_kernel(n, layer, wide, *refs):
+    me = lax.axis_index("head")
+    if wide:
+        (x, w_hbm, rest, gain, after_hbm, out, stream,
+         part, outgoing, arriving, gathered, w, after, load,
+         sum_send, sum_recv, all_send, all_recv) = refs
+        loads = [
+            pltpu.make_async_copy(w_hbm.at[layer], w, load.at[0]),
+            pltpu.make_async_copy(after_hbm, after, load.at[1]),
+        ]
+    else:
+        (x, w_hbm, rest, gain, wq_hbm, wkv_hbm, cos_q, sin_q, cos_kv, sin_kv, q_out, kv_out, stream,
+         part, outgoing, arriving, gathered, w, wq, wkv, load,
+         sum_send, sum_recv, all_send, all_recv) = refs
+        loads = [
+            pltpu.make_async_copy(w_hbm.at[layer], w, load.at[0]),
+            pltpu.make_async_copy(wq_hbm.at[layer + 1], wq, load.at[1]),
+            pltpu.make_async_copy(wkv_hbm.at[layer + 1], wkv, load.at[2]),
+        ]
+    for copy in loads:
+        copy.start()
+    half = part.shape[0] // 2
+    count = half // CHUNK
+    enter(me, n)
+    loads[0].wait()
+    for block in range(0, half, BLOCK):
+        for way in (0, 1):
+            partial_rows(pl.ds(way * half + block, BLOCK), x, w, part)
+    add_rest(me, n, part, rest)
+
+    def place(way, t):
+        return pl.ds(pl.multiple_of(way * half + t * CHUNK, CHUNK), CHUNK)
+
+    def sum_hop(way, t):
+        rows = place(way, t)
+        to = jnp.clip(me - 1 if way == 0 else me + 1, 0, n - 1)
+        return remote(outgoing.at[rows], arriving.at[rows], sum_send.at[way, t],
+                      sum_recv.at[way, t], to)
+
+    def all_hop(way, t):
+        rows = place(way, t)
+        to = jnp.clip(me + 1 if way == 0 else me - 1, 0, n - 1)
+        return remote(gathered.at[rows], gathered.at[rows], all_send.at[way, t],
+                      all_recv.at[way, t], to)
+
+    ends = ((n - 1, 0), (0, n - 1))
+
+    def add_up(t, carry=0):
+        for way in (0, 1):
+            first, owner = ends[way]
+            rows = place(way, t)
+
+            @pl.when(me == first)
+            def _():
+                outgoing[rows, :] = part[rows, :].astype(BF16)
+                sum_hop(way, t).start()
+
+            @pl.when((me != first) & (me != owner))
+            def _():
+                sum_hop(way, t).wait_recv()
+                outgoing[rows, :] = (part[rows, :] + arriving[rows, :].astype(F32)).astype(BF16)
+                sum_hop(way, t).start()
+
+            @pl.when(me == owner)
+            def _():
+                sum_hop(way, t).wait_recv()
+                total = part[rows, :] + arriving[rows, :].astype(F32)
+                stream[pl.ds(pl.multiple_of(t * CHUNK, CHUNK), CHUNK), :] = total
+                gathered[rows, :] = normed_rows(total, gain[...])
+                all_hop(way, t).start()
+
+        return carry
+
+    def hand_on(t, carry=0):
+        for way in (0, 1):
+            first, owner = ends[way]
+
+            @pl.when(me != owner)
+            def _():
+                all_hop(way, t).wait_recv()
+
+                @pl.when(me != first)
+                def _():
+                    all_hop(way, t).start()
+
+        return carry
+
+    def both(t, carry):
+        add_up(t)
+        hand_on(t - LAG)
+        return carry
+
+    def finish(way, block):
+        rows = pl.ds(way * half + block * BLOCK, BLOCK)
+        if wide:
+            widen_rows(rows, gathered, after, out)
+        else:
+            project_rows(rows, gathered, wq, wkv, (cos_q, sin_q, cos_kv, sin_kv), q_out, kv_out)
+
+    lax.fori_loop(0, LAG, add_up, 0)
+    lax.fori_loop(LAG, count, both, 0)
+    for copy in loads[1:]:
+        copy.wait()
+    per = BLOCK // CHUNK
+    waiting = [(way, block) for block in range((count - LAG) // per) for way in (0, 1)]
+    for t in range(count - LAG, count):
+        hand_on(t)
+        if waiting:
+            finish(*waiting.pop(0))
+        if (t + 1) % per == 0:
+            waiting += [(way, t // per) for way in (0, 1)]
+    for item in waiting:
+        finish(*item)
+
+    def drain(t, carry):
+        for way in (0, 1):
+            first, owner = ends[way]
+
+            @pl.when(me != owner)
+            def _():
+                sum_hop(way, t).wait_send()
+
+            @pl.when(me != first)
+            def _():
+                all_hop(way, t).wait_send()
+
+        return carry
+
+    lax.fori_loop(0, count, drain, 0)
+
+
+def scatter_kernel(n, layer, x, w_hbm, rest, out, part, outgoing, arriving, w, load, send, recv):
+    me = lax.axis_index("head")
+    copy = pltpu.make_async_copy(w_hbm.at[layer], w, load.at[0])
+    copy.start()
+    mine = out.shape[0]
+    pieces = mine // CHUNK
+    enter(me, n)
+    copy.wait()
+    for shard in range(n):
+        partial_rows(pl.ds(shard * mine, mine), x, w, part)
+    add_rest(me, n, part, rest)
+
+    def place(at):
+        return pl.ds(pl.multiple_of(at * CHUNK, CHUNK), CHUNK)
+
+    def hop(way, at):
+        rows = place(at)
+        to = jnp.clip(me + 1 if way == 0 else me - 1, 0, n - 1)
+        return remote(outgoing.at[way, rows], arriving.at[way, rows], send.at[way, at],
+                      recv.at[way, at], to)
+
+    def step(i, carry):
+        for way in (0, 1):
+            shard = n - 1 - i // pieces if way == 0 else i // pieces
+            at = shard * pieces + i % pieces
+            rows = place(at)
+            ahead = me < shard if way == 0 else me > shard
+            edge = me == 0 if way == 0 else me == n - 1
+
+            @pl.when(ahead & edge)
+            def _():
+                outgoing[way, rows, :] = part[rows, :].astype(BF16)
+                hop(way, at).start()
+
+            @pl.when(ahead & jnp.logical_not(edge))
+            def _():
+                hop(way, at).wait_recv()
+                outgoing[way, rows, :] = (
+                    part[rows, :] + arriving[way, rows, :].astype(F32)
+                ).astype(BF16)
+                hop(way, at).start()
+
+        return carry
+
+    lax.fori_loop(0, (n - 1) * pieces, step, 0)
+    for piece in range(pieces):
+        at = me * pieces + piece
+        here = slice(piece * CHUNK, (piece + 1) * CHUNK)
+        out[here, :] = part[place(at), :]
+
+        @pl.when(me > 0)
+        def _():
+            hop(0, at).wait_recv()
+            out[here, :] += arriving[0, place(at), :].astype(F32)
+
+        @pl.when(me < n - 1)
+        def _():
+            hop(1, at).wait_recv()
+            out[here, :] += arriving[1, place(at), :].astype(F32)
+
+    def drain(at, carry):
+        shard = at // pieces
+
+        @pl.when(me < shard)
+        def _():
+            hop(0, at).wait_send()
+
+        @pl.when(me > shard)
+        def _():
+            hop(1, at).wait_send()
+
+        return carry
+
+    lax.fori_loop(0, n * pieces, drain, 0)
+
+
+VM = pl.BlockSpec(memory_space=pltpu.VMEM)
+HB = pl.BlockSpec(memory_space=pl.ANY)
+
+
+def parameters(number):
+    return pltpu.CompilerParams(
+        collective_id=number, has_side_effects=True, vmem_limit_bytes=48 * 1024 * 1024
+    )
+
+
+def dma(*shape):
+    return pltpu.SemaphoreType.DMA(shape)
+
+
+def gather_project(n, layer, number, tokens, gain, wq, wkv, tables):
+    mine, width = tokens.shape
+    rows, cq, ck = mine * n, wq.shape[2], wkv.shape[2]
+    return pl.pallas_call(
+        functools.partial(gather_kernel, n, layer),
+        out_shape=[jax.ShapeDtypeStruct((rows, cq), BF16), jax.ShapeDtypeStruct((rows, ck), BF16)],
+        in_specs=[VM, VM, HB, HB] + [VM] * 4,
+        out_specs=[VM, VM],
+        scratch_shapes=[
+            pltpu.VMEM((rows, width), BF16),
+            pltpu.VMEM(wq.shape[1:], BF16),
+            pltpu.VMEM(wkv.shape[1:], BF16),
+            dma(2),
+            dma(2, rows // CHUNK),
+            dma(2, rows // CHUNK),
+        ],
+        compiler_params=parameters(number),
+        name="gather_project",
+    )(tokens, gain, wq, wkv, *tables)
+
+
+def exchange(n, layer, number, x, w, rest, gain, after, tables=None):
+    rows, width = x.shape[0], w.shape[2]
+    half = rows // 2
+    wide = tables is None
+    count = half // CHUNK
+    if wide:
+        outs = [jax.ShapeDtypeStruct((rows, after[0].shape[2]), BF16)]
+        kept = [pltpu.VMEM(after[0].shape, BF16)]
+    else:
+        outs = [jax.ShapeDtypeStruct((rows, part.shape[2]), BF16) for part in after]
+        kept = [pltpu.VMEM(part.shape[1:], BF16) for part in after]
+    outs.append(jax.ShapeDtypeStruct((half, width), F32))
+    more = () if wide else tables
+    return pl.pallas_call(
+        functools.partial(exchange_kernel, n, layer, wide),
+        out_shape=outs,
+        in_specs=[VM, HB, VM, VM] + [HB] * len(after) + [VM] * len(more),
+        out_specs=[VM] * len(outs),
+        scratch_shapes=[
+            pltpu.VMEM((rows, width), F32),
+            pltpu.VMEM((rows, width), BF16),
+            pltpu.VMEM((rows, width), BF16),
+            pltpu.VMEM((rows, width), BF16),
+            pltpu.VMEM(w.shape[1:], BF16),
+            *kept,
+            dma(3),
+            dma(2, count),
+            dma(2, count),
+            dma(2, count),
+            dma(2, count),
+        ],
+        compiler_params=parameters(number),
+        name="exchange",
+    )(x, w, rest, gain, *after, *more)
+
+
+def scatter(n, layer, number, x, w, rest):
+    rows, width = x.shape[0], w.shape[2]
+    return pl.pallas_call(
+        functools.partial(scatter_kernel, n, layer),
+        out_shape=jax.ShapeDtypeStruct((rows // n, width), F32),
+        in_specs=[VM, HB, VM],
+        out_specs=VM,
+        scratch_shapes=[
+            pltpu.VMEM((rows, width), F32),
+            pltpu.VMEM((2, rows, width), BF16),
+            pltpu.VMEM((2, rows, width), BF16),
+            pltpu.VMEM(w.shape[1:], BF16),
+            dma(1),
+            dma(2, rows // CHUNK),
+            dma(2, rows // CHUNK),
+        ],
+        compiler_params=parameters(number),
+        name="scatter",
+    )(x, w, rest)
+
+
+def lane_tables():
+    freq = 500000.0 ** (-(np.arange(HD // 2) * 2.0 / HD))
+    angle = np.arange(SEG_LEN)[:, None] * freq[None, :]
+    c, s = np.cos(angle), np.sin(angle)
+    cosine, sine = np.concatenate([c, c], 1), np.concatenate([-s, s], 1)
+    tables = (
+        np.concatenate([cosine, cosine], 1),
+        np.concatenate([sine, sine], 1),
+        np.concatenate([cosine, np.ones_like(cosine)], 1),
+        np.concatenate([sine, np.zeros_like(sine)], 1),
+    )
+    return tuple(jnp.asarray(table, F32) for table in tables)
 
 
 def prefix(x, axis, combine, identity):
@@ -25,29 +525,6 @@
         return jax.tree.map(lambda a, b: jnp.where(reached, a, b), new, before)
 
     return lax.fori_loop(0, count, hop, start)
-
-
-def rms_norm(value, gain):
-    factor = lax.rsqrt(jnp.mean(value * value, axis=-1, keepdims=True) + 1e-05)
-    return (value * factor * gain).astype(jnp.bfloat16)
-
-
-def rope_tables(position):
-    half = HD // 2
-    freq = 500000.0 ** (-(jnp.arange(half).astype(jnp.float32) * 2.0 / HD))
-    angle = position.astype(jnp.float32)[:, None] * freq[None, :]
-    return (jnp.cos(angle), jnp.sin(angle))
-
-
-def rotate(tensor, cosine, sine):
-    half = tensor.shape[-1] // 2
-    first = tensor[..., :half]
-    second = tensor[..., half:]
-    cos_part = cosine[:, None, :]
-    sin_part = sine[:, None, :]
-    return jnp.concatenate(
-        [first * cos_part - second * sin_part, second * cos_part + first * sin_part], axis=-1
-    )
 
 
 def combine(earlier, later):
@@ -76,32 +553,17 @@
     group = HEADS // KV_HEADS
     local_kv = local_heads // group
     scale = HD ** (-0.5)
-    cosine, sine = rope_tables(jnp.arange(rows_all) % SEG_LEN)
+    tables = lane_tables()
+    n = lax.axis_size("head")
     docs = document_index.reshape(seg_local, SEG_LEN)
     causal = jnp.arange(SEG_LEN)[:, None] >= jnp.arange(SEG_LEN)[None, :]
-    stream = tokens
+    rest = tokens
+    query, pairs = gather_project(n, 0, 0, tokens, attn_gain[:1], w_query, w_kv, tables)
     stored = []
     for layer in range(DEPTH_NUMBER):
-        query_weight = w_query[layer]
-        pair_weight = w_kv[layer]
-        out_weight = w_out[layer]
-        widening_matrix = w_gate_up[layer]
-        down_weight = w_down[layer]
-        normed = rms_norm(stream, attn_gain[layer])
-        project_piece = lax.all_gather(normed, "head", axis=0, tiled=True)
-        projected = jnp.concatenate(
-            [
-                jnp.dot(project_piece, query_weight, preferred_element_type=jnp.float32),
-                jnp.dot(project_piece, pair_weight, preferred_element_type=jnp.float32),
-            ],
-            axis=1,
-        )
-        query = rotate(
-            projected[:, :cols_query].reshape(rows_all, local_heads, HD), cosine, sine
-        ).astype(jnp.bfloat16)
-        pairs = projected[:, cols_query:].reshape(rows_all, local_kv, 2, HD)
-        lookup_vectors = rotate(pairs[:, :, 0], cosine, sine).astype(jnp.bfloat16)
-        values = pairs[:, :, 1].astype(jnp.bfloat16)
+        pairs = pairs.reshape(rows_all, local_kv, 2, HD)
+        lookup_vectors = pairs[:, :, 0]
+        values = pairs[:, :, 1]
         query = query.reshape(seg_local, SEG_LEN, local_kv, group, HD)
         lookup_vectors = lookup_vectors.reshape(seg_local, SEG_LEN, local_kv, HD)
         values = values.reshape(seg_local, SEG_LEN, local_kv, HD)
@@ -159,27 +621,17 @@
         )
         outputs = result.reshape(SEG_LEN, cols_query).astype(jnp.bfloat16)
         stored.append(jnp.stack(after_list))
-        mixed = lax.psum_scatter(
-            jnp.dot(outputs, out_weight, preferred_element_type=jnp.float32),
-            "head",
-            scatter_dimension=0,
-            tiled=True,
+        widening = jnp.swapaxes(w_gate_up[layer], 0, 1)
+        inner, rest = exchange(
+            n, layer, 1 + 2 * layer, outputs, w_out, rest, mlp_gain[layer : layer + 1], (widening,)
         )
-        middle = stream + mixed
-        both = jnp.einsum(
-            "rd,dtf->rtf",
-            lax.all_gather(rms_norm(middle, mlp_gain[layer]), "head", axis=0, tiled=True),
-            widening_matrix,
-            preferred_element_type=jnp.float32,
-        )
-        inner = (jax.nn.silu(both[:, 0]) * both[:, 1]).astype(jnp.bfloat16)
-        down = lax.psum_scatter(
-            jnp.dot(inner, down_weight, preferred_element_type=jnp.float32),
-            "head",
-            scatter_dimension=0,
-            tiled=True,
-        )
-        stream = middle + down
+        if layer + 1 < DEPTH_NUMBER:
+            query, pairs, rest = exchange(
+                n, layer, 2 + 2 * layer, inner, w_down, rest, attn_gain[layer + 1 : layer + 2],
+                (w_query, w_kv), tables,
+            )
+        else:
+            stream = scatter(n, layer, 2 + 2 * layer, inner, w_down, rest)
     return (stream, jnp.stack(stored))
 
 

time: 657 us -> 1070 us (1.63)
  Pallas kernels: 0 us -> 913 us
  waiting for transfers between devices: 461 us -> 0.82 us
  matrix products: 66.4 us -> 19.1 us
  local copies, waits for them, and re-layouts: 37.8 us -> 48.6 us
    pallas_call x0 -> x5, Pallas kernels: none -> 913 us  [the longest x3 815 us: exchange(): pl.pallas_call(functools.partial(exchange_kernel, n, layer, wide), out_sh...]
    reduce_scatter x4 -> x0, waiting for transfers between devices: 305 us -> none  [the longest x2 153 us: body(): lax.psum_scatter(jnp.dot(inner, down_weight, preferred_element_type=jnp.f...]
    all_gather x4 -> x0, waiting for transfers between devices: 155 us -> none  [the longest x2 80.7 us: body(): project_piece = lax.all_gather(normed, 'head', axis=0, tiled=True)]
    dot_general x10 -> x0, matrix products: 51.2 us -> none  [the longest x2 16.6 us: body(): jnp.einsum('rd,dtf->rtf', lax.all_gather(rms_norm(middle, mlp_gain[layer]...]
    dot_general x6 -> x0, local copies, waits for them, and re-layouts: 14.9 us -> none  [the longest x3 12.5 us: body(): jnp.dot(project_piece, query_weight, preferred_element_type=jnp.float32)]
    unnamed x61 -> x84, local copies, waits for them, and re-layouts: 4.56 us -> 18.4 us
  transfers between devices with their start and end apart: 10 -> 2, of which waited for: 8 -> 1; matrix products, arithmetic and copies ran while one was open for 10% -> 5% of each run, Pallas kernels for 0% -> 0%
where the time goes in v1:
time: 1070 us; the launch traced here: 1060 us
  Pallas kernels  913 us (85%)
  local copies, waits for them, and re-layouts  48.6 us (5%)
  other arithmetic  48 us (4%)
  blocking collectives  20.2 us (2%)
  matrix products  19.1 us (2%)
  between operations  15.1 us (1%)
    pallas_call x3, Pallas kernels, exchange(): pl.pallas_call(functools.partial(exchange_kernel, n, layer, wide), out_sh...  815 us
    pallas_call x1, Pallas kernels, scatter(): pl.pallas_call(functools.partial(scatter_kernel, n, layer), out_shape=jax...  61.7 us
    pallas_call x1, Pallas kernels, gather_project(): pl.pallas_call(functools.partial(gather_kernel, n, layer), out_shape=[jax...  36.1 us
    select_n x32, other arithmetic, hop(): return jax.tree.map(lambda a, b: jnp.where(reached, a, b), new, before)  29.5 us
  transfers between devices with their start and end apart: 2, of which 1 were waited for; matrix products, arithmetic and copies ran while one was open for 5% of the time, Pallas kernels for 0%

profile of v1, /device:TPU:16, one launch (start us, length us, event | category | flops | bytes accessed | tf_op | source)
XLA Modules:
  0.0 1064.9 jit_solution(15933326823044450291)
XLA Ops:
  8.0 1.6 copy-done
  14.6 36.1 %gather_project.1 = (bf16[512,512]{1,0:T(8,128)(2,1)S(1)}, bf16[512,256]{1,0:T(8,128)(2,1)S(1)}) custom-call(f32[128,2048]{1,0:T(8,128)S(1)} %copy-done.1, f32[1,2048]{1,0:T(1,128)S(1)} %get-tuple-element.331.gain, bf16[2,2048,512]{2,1,0:T(8,128)(2,1)} %refs_4_.1, bf16[2,2048,256]{2,1,0:T(8,128)(2,1)S(1)} %copy-done, f32[512,128]{1,0:T(8,128)S(1)} %copy-done.4, ...), custom_call_target="tpu_custom_call" | custom-call | tf_op jit(solution)/shard_map/gather_project/pallas_call | solution.py:426
  54.9 10.0 all_gather.15
  67.9 1.5 fusion.50
  70.8 4.6 divide_convert_fusion.1
  75.4 4.4 fusion.14
  80.7 13.1 %fusion.44 = (bf16[1,2048,2,1024]{3,2,1,0:T(2,128)(2,1)S(1)}, bf16[1,2048,2,1024]{3,2,1,0:T(2,128)(2,1)S(1)}) fusion(bf16[2,2048,2,1024]{3,2,1,0:T(2,128)(2,1)} %param.32), kind=kLoop, calls=%fused_computation.87 | loop fusion | bytes 33554432 | tf_op jit(solution)/shard_map/slice | solution.py:624
  93.8 9.6 copy_bitcast_fusion
  103.4 15.0 %while.32 = (s32[]{:T(128)}, f32[1,512]{1,0:T(1,128)S(1)}, f32[128,512]{1,0:T(8,128)S(1)}, s32[]{:T(128)}, f32[8,1,512]{2,1,0:T(1,128)}, /*index=5*/f32[8,128,512]{2,1,0:T(8,128)}, s32[]{:T(128)}, s32[]{:T(128)}) while((s32[]{:T(128)}, f32[1,512]{1,0:T(1,128)S(1)}, f32[128,512]{1,0:T(8,128)S(1)}, s32[]{:T(128)}, ...), condition=%wide.region_3.4_spmd.clone, body=%wide.region_2.3_spmd.clone.sunk | while | flops 263684 | bytes 796787 | solution.py:527
  119.5 1.8 fusion.22
  121.7 270.2 %exchange.3 = (bf16[512,1024]{1,0:T(8,128)(2,1)S(1)}, f32[256,2048]{1,0:T(8,128)S(1)}) custom-call(bf16[512,512]{1,0:T(8,128)(2,1)S(1)} %copy.87.refs_0_, bf16[2,512,2048]{2,1,0:T(8,128)(2,1)} %refs_1_.5, f32[128,2048]{1,0:T(8,128)S(1)} %copy-done.2, f32[1,2048]{1,0:T(1,128)S(1)} %get-tuple-element.329.refs_3_, bf16[2,2048,1024]{2,1,0:T(8,128)(2,1)} %get-tuple-element.351.refs_4_), custom_call_target="tpu_custom_call" | custom-call | tf_op jit(solution)/shard_map/exchange/pallas_call | solution.py:457
  393.2 272.9 %exchange.4 = (bf16[512,512]{1,0:T(8,128)(2,1)S(1)}, bf16[512,256]{1,0:T(8,128)(2,1)S(1)}, f32[256,2048]{1,0:T(8,128)S(1)}) custom-call(bf16[512,1024]{1,0:T(8,128)(2,1)S(1)} %get-tuple-element.235.refs_0_, bf16[2,1024,2048]{2,1,0:T(8,128)(2,1)} %w_hbm.1, f32[256,2048]{1,0:T(8,128)} %copy-done.3, f32[1,2048]{1,0:T(1,128)S(1)} %get-tuple-element.330.refs_3_, ...), custom_call_target="tpu_custom_call" | custom-call | tf_op jit(solution)/shard_map/exchange/pallas_call | solution.py:457
  671.7 1.8 copy.118
  673.5 10.1 all_gather.14
  684.6 1.5 fusion.51
  686.2 2.9 fusion.52
  689.1 3.2 copy-done.12
  693.7 5.2 divide_convert_fusion
  699.0 2.4 copy-done.13
  701.4 1.8 fusion.17
  704.0 14.9 %while.33 = (s32[]{:T(128)}, f32[1,512]{1,0:T(1,128)S(1)}, f32[128,512]{1,0:T(8,128)S(1)}, s32[]{:T(128)}, f32[8,1,512]{2,1,0:T(1,128)}, /*index=5*/f32[8,128,512]{2,1,0:T(8,128)}, s32[]{:T(128)}, s32[]{:T(128)}) while((s32[]{:T(128)}, f32[1,512]{1,0:T(1,128)S(1)}, f32[128,512]{1,0:T(8,128)S(1)}, s32[]{:T(128)}, ...), condition=%wide.region_10.11_spmd.clone, body=%wide.region_9.10_spmd.clone.sunk | while | flops 263684 | bytes 796787 | solution.py:527
  721.0 1.8 fusion.23
  723.1 271.9 %exchange.5 = (bf16[512,1024]{1,0:T(8,128)(2,1)S(1)}, f32[256,2048]{1,0:T(8,128)S(1)}) custom-call(bf16[512,512]{1,0:T(8,128)(2,1)S(1)} %copy.100.refs_0_, bf16[2,512,2048]{2,1,0:T(8,128)(2,1)} %refs_1_.5, f32[256,2048]{1,0:T(8,128)S(1)} %get-tuple-element.241.refs_2_, f32[1,2048]{1,0:T(1,128)S(1)} %get-tuple-element.328.refs_3_, ...), custom_call_target="tpu_custom_call" | custom-call | tf_op jit(solution)/shard_map/exchange/pallas_call | solution.py:457
  995.0 61.7 %scatter.1 = f32[128,2048]{1,0:T(8,128)S(1)} custom-call(bf16[512,1024]{1,0:T(8,128)(2,1)S(1)} %get-tuple-element.242.x, bf16[2,1024,2048]{2,1,0:T(8,128)(2,1)} %w_hbm.1, f32[256,2048]{1,0:T(8,128)S(1)} %get-tuple-element.243.rest), custom_call_target="tpu_custom_call" | custom-call | tf_op jit(solution)/shard_map/scatter/pallas_call | solution.py:482
  (166 shorter events, 59.4 us)
Async XLA Ops:
  7.2 96.2 %all-gather.3.cloned.1.call-start = ((), (), s32[]{:S(2)}) async-start(), calls=%async_computation | async-start | bytes 2359296 | tf_op jit(solution)/shard_map/all_gather | solution.py:517
  14.6 36.2 %copy-start.24 = (bf16[2,128,512]{2,1,0:T(8,128)(2,1)S(1)}, bf16[2,128,512]{2,1,0:T(8,128)(2,1)}, u32[]{:S(2)}) copy-start(bf16[2,128,512]{2,1,0:T(8,128)(2,1)} %param.24) | copy-start | bytes 786436
  52.5 12.5 %copy-start.22 = (f32[2,128,512]{2,1,0:T(8,128)S(1)}, f32[2,128,512]{2,1,0:T(8,128)}, u32[]{:S(2)}) copy-start(f32[2,128,512]{2,1,0:T(8,128)} %param.25) | copy-start | bytes 1572868
  52.6 14.3 %copy-start.36 = (s32[1,4,4]{2,1,0:T(4,128)S(1)}, s32[1,4,4]{2,1,0:T(4,128)}, u32[]{:S(2)}) copy-start(s32[1,4,4]{2,1,0:T(4,128)} %param.23) | copy-start | bytes 196
  53.1 14.5 %copy-start.16 = (f32[2,64,4,128]{3,1,2,0:T(8,128)}, f32[2,64,4,128]{3,1,2,0:T(8,128)S(1)}, u32[]{:S(2)}) copy-start(f32[2,64,4,128]{3,1,2,0:T(8,128)S(1)} %fusion.28) | copy-start | bytes 786436
  53.1 14.5 %copy-start.35 = (s32[512]{0:T(512)S(1)}, s32[512]{0:T(512)}, u32[]{:S(2)}) copy-start(s32[512]{0:T(512)} %param.22) | copy-start | bytes 6148
  54.0 13.5 %copy-start.32 = (f32[512]{0:T(512)}, f32[512]{0:T(512)S(1)}, u32[]{:S(2)}) copy-start(f32[512]{0:T(512)S(1)} %broadcast_in_dim.47) | copy-start | bytes 6148
  54.0 15.3 %copy-start.29 = (f32[512]{0:T(512)}, f32[512]{0:T(512)S(1)}, u32[]{:S(2)}) copy-start(f32[512]{0:T(512)S(1)} %get-tuple-element.335) | copy-start | bytes 6148
  54.8 649.2 %all-gather.5.cloned.1.call-start = ((), (), s32[]{:S(2)}) async-start(), calls=%async_computation.1 | async-start | bytes 2359296 | tf_op jit(solution)/shard_map/all_gather | solution.py:517
  80.0 13.8 %copy-start.26 = (f32[8,64]{1,0:T(8,128)}, f32[8,64]{1,0:T(8,128)S(1)}, u32[]{:S(2)}) copy-start(f32[8,64]{1,0:T(8,128)S(1)} %broadcast_in_dim.42) | copy-start | bytes 6148
  80.1 13.7 %copy-start.31 = (f32[512]{0:T(512)}, f32[512]{0:T(512)S(1)}, u32[]{:S(2)}) copy-start(f32[512]{0:T(512)S(1)} %broadcast_in_dim.44) | copy-start | bytes 6148
  93.8 9.6 copy-start.25
  93.8 24.7 %copy-start.17 = (f32[2,64,4,128]{3,1,2,0:T(8,128)S(1)}, f32[2,64,4,128]{3,1,2,0:T(8,128)}, u32[]{:S(2)}) copy-start(f32[2,64,4,128]{3,1,2,0:T(8,128)} %copy-done.16) | copy-start | bytes 786436
  93.8 24.7 %copy-start.18 = (f32[1,128,512]{1,2,0:T(8,128)S(1)}, f32[1,128,512]{1,2,0:T(8,128)}, u32[]{:S(2)}) copy-start(f32[1,128,512]{1,2,0:T(8,128)} %copy.114) | copy-start | bytes 786436
  93.8 24.7 %copy-start.30 = (f32[512]{0:T(512)S(1)}, f32[512]{0:T(512)}, u32[]{:S(2)}) copy-start(f32[512]{0:T(512)} %copy-done.29) | copy-start | bytes 6148
  93.8 24.7 %copy-start.33 = (f32[512]{0:T(512)S(1)}, f32[512]{0:T(512)}, u32[]{:S(2)}) copy-start(f32[512]{0:T(512)} %copy-done.32) | copy-start | bytes 6148
  103.4 18.2 %copy-start.2 = (f32[128,2048]{1,0:T(8,128)S(1)}, f32[128,2048]{1,0:T(8,128)}, u32[]{:S(2)}) copy-start(f32[128,2048]{1,0:T(8,128)} %refs_2_.1) | copy-start | bytes 3145732
  121.6 271.6 %copy-start.5 = (f32[512,128]{1,0:T(8,128)S(1)}, f32[512,128]{1,0:T(8,128)}, u32[]{:S(2)}) copy-start(f32[512,128]{1,0:T(8,128)} %constant.75.clone.cos_q.refs_6_) | copy-start | bytes 786436
  121.6 271.6 %copy-start.7 = (f32[512,128]{1,0:T(8,128)S(1)}, f32[512,128]{1,0:T(8,128)}, u32[]{:S(2)}) copy-start(f32[512,128]{1,0:T(8,128)} %constant.76.clone.sin_q.refs_7_) | copy-start | bytes 786436
  121.6 271.6 %copy-start.9 = (f32[512,128]{1,0:T(8,128)S(1)}, f32[512,128]{1,0:T(8,128)}, u32[]{:S(2)}) copy-start(f32[512,128]{1,0:T(8,128)} %constant.77.clone.cos_kv.refs_8_) | copy-start | bytes 786436
  121.6 271.6 %copy-start.11 = (f32[512,128]{1,0:T(8,128)S(1)}, f32[512,128]{1,0:T(8,128)}, u32[]{:S(2)}) copy-start(f32[512,128]{1,0:T(8,128)} %constant.78.clone.sin_kv.refs_9_) | copy-start | bytes 786436
  701.4 17.6 %copy-start.19 = (f32[2,64,4,128]{3,1,2,0:T(8,128)S(1)}, f32[2,64,4,128]{3,1,2,0:T(8,128)}, u32[]{:S(2)}) copy-start(f32[2,64,4,128]{3,1,2,0:T(8,128)} %fusion.26) | copy-start | bytes 786436
  701.4 17.6 %copy-start.20 = (f32[1,128,512]{1,2,0:T(8,128)S(1)}, f32[1,128,512]{1,2,0:T(8,128)}, u32[]{:S(2)}) copy-start(f32[1,128,512]{1,2,0:T(8,128)} %copy.118) | copy-start | bytes 786436
  703.2 16.8 %copy-start.21 = (f32[128,512]{0,1:T(8,128)S(1)}, f32[128,512]{0,1:T(8,128)}, u32[]{:S(2)}) copy-start(f32[128,512]{0,1:T(8,128)} %get-tuple-element.320) | copy-start | bytes 786436
  (17 other events, 39.4 us)
Sparse Core Ops, SparseCore 0:
  54.9 30.6 all-gather.2
  671.2 32.7 all-gather.4

commit v2 on v1

--- a/solution.py
+++ b/solution.py
@@ -16,7 +16,7 @@
 BLOCK = 128
 DEPTH_NUMBER = 2
 CHUNK = 32
-LAG = 4
+LAG = 2
 MESH = pl.DeviceIdType.MESH
 F32 = jnp.float32
 BF16 = jnp.bfloat16
@@ -246,72 +246,81 @@
 
     ends = ((n - 1, 0), (0, n - 1))
 
-    def add_up(t, carry=0):
-        for way in (0, 1):
-            first, owner = ends[way]
-            rows = place(way, t)
-
-            @pl.when(me == first)
-            def _():
-                outgoing[rows, :] = part[rows, :].astype(BF16)
-                sum_hop(way, t).start()
-
-            @pl.when((me != first) & (me != owner))
-            def _():
-                sum_hop(way, t).wait_recv()
-                outgoing[rows, :] = (part[rows, :] + arriving[rows, :].astype(F32)).astype(BF16)
-                sum_hop(way, t).start()
-
-            @pl.when(me == owner)
-            def _():
-                sum_hop(way, t).wait_recv()
-                total = part[rows, :] + arriving[rows, :].astype(F32)
-                stream[pl.ds(pl.multiple_of(t * CHUNK, CHUNK), CHUNK), :] = total
-                gathered[rows, :] = normed_rows(total, gain[...])
+    def add_up(way, t):
+        first, owner = ends[way]
+        rows = place(way, t)
+
+        @pl.when(me == first)
+        def _():
+            outgoing[rows, :] = part[rows, :].astype(BF16)
+            sum_hop(way, t).start()
+
+        @pl.when((me != first) & (me != owner))
+        def _():
+            sum_hop(way, t).wait_recv()
+            outgoing[rows, :] = (part[rows, :] + arriving[rows, :].astype(F32)).astype(BF16)
+            sum_hop(way, t).start()
+
+        @pl.when(me == owner)
+        def _():
+            sum_hop(way, t).wait_recv()
+            total = part[rows, :] + arriving[rows, :].astype(F32)
+            stream[pl.ds(pl.multiple_of(t * CHUNK, CHUNK), CHUNK), :] = total
+            gathered[rows, :] = normed_rows(total, gain[...])
+            all_hop(way, t).start()
+
+    def hand_on(way, t):
+        first, owner = ends[way]
+
+        @pl.when(me != owner)
+        def _():
+            all_hop(way, t).wait_recv()
+
+            @pl.when(me != first)
+            def _():
                 all_hop(way, t).start()
 
-        return carry
-
-    def hand_on(t, carry=0):
-        for way in (0, 1):
-            first, owner = ends[way]
-
-            @pl.when(me != owner)
-            def _():
-                all_hop(way, t).wait_recv()
-
-                @pl.when(me != first)
-                def _():
-                    all_hop(way, t).start()
-
-        return carry
-
-    def both(t, carry):
-        add_up(t)
-        hand_on(t - LAG)
-        return carry
-
     def finish(way, block):
-        rows = pl.ds(way * half + block * BLOCK, BLOCK)
+        rows = pl.ds(pl.multiple_of(way * half + block * BLOCK, BLOCK), BLOCK)
         if wide:
             widen_rows(rows, gathered, after, out)
         else:
             project_rows(rows, gathered, wq, wkv, (cos_q, sin_q, cos_kv, sin_kv), q_out, kv_out)
 
-    lax.fori_loop(0, LAG, add_up, 0)
-    lax.fori_loop(LAG, count, both, 0)
-    for copy in loads[1:]:
-        copy.wait()
     per = BLOCK // CHUNK
-    waiting = [(way, block) for block in range((count - LAG) // per) for way in (0, 1)]
-    for t in range(count - LAG, count):
-        hand_on(t)
-        if waiting:
-            finish(*waiting.pop(0))
-        if (t + 1) % per == 0:
-            waiting += [(way, t // per) for way in (0, 1)]
-    for item in waiting:
-        finish(*item)
+
+    def tick(now, carry):
+        down, back = [], []
+        for way in (0, 1):
+            far = n - 1 - me if way == 0 else me
+            down.append(now - LAG * far)
+            back.append(now - LAG * (n - 1) - LAG * (n - 1 - far))
+        for way in (0, 1):
+
+            @pl.when((down[way] >= 0) & (down[way] < count))
+            def _():
+                add_up(way, down[way])
+
+        for way in (0, 1):
+
+            @pl.when((back[way] >= 0) & (back[way] < count))
+            def _():
+                hand_on(way, back[way])
+
+        @pl.when(now == LAG * (n - 1))
+        def _():
+            for copy in loads[1:]:
+                copy.wait()
+
+        for way in (0, 1):
+
+            @pl.when((back[way] >= 0) & (back[way] < count) & (back[way] % per == per - 1))
+            def _():
+                finish(way, back[way] // per)
+
+        return carry
+
+    lax.fori_loop(0, 2 * LAG * (n - 1) + count, tick, 0)
 
     def drain(t, carry):
         for way in (0, 1):
@@ -512,23 +521,171 @@
     return tuple(jnp.asarray(table, F32) for table in tables)
 
 
-def prefix(x, axis, combine, identity):
-    count, here = (lax.axis_size(axis), lax.axis_index(axis))
-    everything = jax.tree.map(lambda part: lax.all_gather(part, axis), x)
-    start = jax.tree.map(
-        lambda part, zero: jnp.broadcast_to(jnp.asarray(zero, part.dtype), part.shape), x, identity
-    )
-
-    def hop(k, before):
-        reached = k < here
-        new = combine(before, jax.tree.map(lambda part: part[k], everything))
-        return jax.tree.map(lambda a, b: jnp.where(reached, a, b), new, before)
-
-    return lax.fori_loop(0, count, hop, start)
-
-
-def combine(earlier, later):
-    return (earlier[0] * later[0], later[0] * earlier[1] + later[1])
+def heads_dot(a, b):
+    return lax.dot_general(a, b, (((1,), (1,)), ((), ())), preferred_element_type=F32)
+
+
+def attend_kernel(count, query, pairs, slots, bias, initial, weight, keep, rate, out, after,
+                  written, box, probs, state, send, recv):
+    me = lax.axis_index("seg")
+    group = HEADS // KV_HEADS
+    local_kv = pairs.shape[1] // (2 * HD)
+    span = group * HD
+    scale = HD ** (-0.5)
+    barrier = pltpu.get_barrier_semaphore()
+
+    def greet(k, carry):
+        @pl.when(k != me)
+        def _():
+            pl.semaphore_signal(barrier, inc=1, device_id={"seg": k}, device_id_type=MESH)
+
+        return carry
+
+    lax.fori_loop(0, count, greet, 0)
+
+    for g in range(local_kv):
+        keys = pairs[:, 2 * g * HD : (2 * g + 1) * HD]
+        values = pairs[:, (2 * g + 1) * HD : (2 * g + 2) * HD]
+        stacked = jnp.concatenate(
+            [slots[:, g * span + h * HD : g * span + (h + 1) * HD] for h in range(group)], axis=0
+        )
+        scores = heads_dot(stacked, keys) * scale
+        top = jnp.exp(scores - jnp.max(scores, axis=-1, keepdims=True))
+        share = (top / jnp.sum(top, axis=-1, keepdims=True)).astype(BF16)
+        fresh = jnp.dot(share, values, preferred_element_type=F32)
+        written[:, g * span : (g + 1) * span] = jnp.concatenate(
+            [fresh[h * MEM : (h + 1) * MEM] for h in range(group)], axis=1
+        )
+    box[me] = written[...].astype(BF16)
+    pl.semaphore_wait(barrier, count - 1)
+
+    def hop(source, target):
+        return pltpu.make_async_remote_copy(
+            src_ref=box.at[source],
+            dst_ref=box.at[source],
+            send_sem=send.at[target],
+            recv_sem=recv.at[source],
+            device_id={"seg": target},
+            device_id_type=MESH,
+        )
+
+    def post(k, carry):
+        @pl.when(k > me)
+        def _():
+            hop(me, k).start()
+
+        return carry
+
+    lax.fori_loop(0, count, post, 0)
+    blocks = query.shape[0] // BLOCK
+    for g in range(local_kv):
+        for b in range(blocks):
+            rows, reach = slice(b * BLOCK, (b + 1) * BLOCK), (b + 1) * BLOCK
+            parts = [
+                query[rows, g * span + h * HD : g * span + (h + 1) * HD] for h in range(group)
+            ]
+            slot_scores = jnp.concatenate(
+                [
+                    heads_dot(parts[h], slots[:, g * span + h * HD : g * span + (h + 1) * HD])
+                    for h in range(group)
+                ],
+                axis=0,
+            ) * scale
+            shade = bias[rows, :reach]
+            token_scores = heads_dot(
+                jnp.concatenate(parts, axis=0), pairs[:reach, 2 * g * HD : (2 * g + 1) * HD]
+            ) * scale + jnp.concatenate([shade] * group, axis=0)
+            peak = jnp.maximum(
+                jnp.max(slot_scores, axis=-1, keepdims=True),
+                jnp.max(token_scores, axis=-1, keepdims=True),
+            )
+            slot_top = jnp.exp(slot_scores - peak)
+            token_top = jnp.exp(token_scores - peak)
+            total = jnp.sum(slot_top, axis=-1, keepdims=True) + jnp.sum(
+                token_top, axis=-1, keepdims=True
+            )
+            inverse = 1.0 / total
+            probs[g, b, :, :MEM] = (slot_top * inverse).astype(BF16)
+            probs[g, b, :, MEM : MEM + reach] = (token_top * inverse).astype(BF16)
+    state[...] = keep[...] * initial[...]
+
+    def take(k, carry):
+        @pl.when(k < me)
+        def _():
+            hop(k, me).wait_recv()
+            state[...] += weight[k] * box[k].astype(F32)
+
+        return carry
+
+    lax.fori_loop(0, count, take, 0)
+    after[...] = rate[...] * state[...] + (1.0 - rate[...]) * written[...]
+    for g in range(local_kv):
+        memory = state[:, g * span : (g + 1) * span].astype(BF16)
+        for b in range(blocks):
+            reach = (b + 1) * BLOCK
+            found = jnp.dot(
+                probs[g, b, :, MEM : MEM + reach],
+                pairs[:reach, (2 * g + 1) * HD : (2 * g + 2) * HD],
+                preferred_element_type=F32,
+            )
+            pieces = [
+                found[h * BLOCK : (h + 1) * BLOCK]
+                + jnp.dot(
+                    probs[g, b, h * BLOCK : (h + 1) * BLOCK, :MEM],
+                    memory[:, h * HD : (h + 1) * HD],
+                    preferred_element_type=F32,
+                )
+                for h in range(group)
+            ]
+            out[b * BLOCK : (b + 1) * BLOCK, g * span : (g + 1) * span] = jnp.concatenate(
+                pieces, axis=1
+            ).astype(BF16)
+
+    def drain(k, carry):
+        @pl.when(k > me)
+        def _():
+            hop(me, k).wait_send()
+
+        return carry
+
+    lax.fori_loop(0, count, drain, 0)
+
+
+def attend(count, number, query, pairs, slots, bias, initial, weight, keep, rate):
+    rows, columns = query.shape
+    local_kv = pairs.shape[1] // (2 * HD)
+    group = HEADS // KV_HEADS
+    return pl.pallas_call(
+        functools.partial(attend_kernel, count),
+        out_shape=[
+            jax.ShapeDtypeStruct((rows, columns), BF16),
+            jax.ShapeDtypeStruct((MEM, columns), F32),
+        ],
+        in_specs=[VM] * 8,
+        out_specs=[VM, VM],
+        scratch_shapes=[
+            pltpu.VMEM((MEM, columns), F32),
+            pltpu.VMEM((count, MEM, columns), BF16),
+            pltpu.VMEM((local_kv, rows // BLOCK, group * BLOCK, MEM + rows), BF16),
+            pltpu.VMEM((MEM, columns), F32),
+            dma(count),
+            dma(count),
+        ],
+        compiler_params=parameters(number),
+        name="attend",
+    )(query, pairs, slots, bias, initial, weight, keep, rate)
+
+
+def carry_weights(retain):
+    count, here = lax.axis_size("seg"), lax.axis_index("seg")
+    rates = lax.all_gather(retain[:, 0], "seg")
+    at = jnp.arange(count)
+    between = (at[None, :] > at[:, None]) & (at[None, :] < here)
+    keep = jnp.prod(jnp.where(between[:, :, None, None], rates[None], 1.0), axis=1)
+    weight = jnp.where((at < here)[:, None, None], (1.0 - rates) * keep, 0.0)
+    whole = jnp.prod(jnp.where((at < here)[:, None, None], rates, 1.0), axis=0)
+    weight = jnp.repeat(weight.transpose(1, 0, 2), HD, axis=2)[:, :, None, :]
+    return weight, jnp.repeat(whole, HD, axis=1)[:, None, :], jnp.repeat(retain, HD, axis=2)
 
 
 def body(
@@ -546,84 +703,25 @@
     w_gate_up,
     w_down,
 ):
-    seg_local = document_index.shape[0] // SEG_LEN
-    rows_all = seg_local * SEG_LEN
-    cols_query = w_query.shape[2]
-    local_heads = cols_query // HD
-    group = HEADS // KV_HEADS
-    local_kv = local_heads // group
-    scale = HD ** (-0.5)
+    n, count = lax.axis_size("head"), lax.axis_size("seg")
     tables = lane_tables()
-    n = lax.axis_size("head")
-    docs = document_index.reshape(seg_local, SEG_LEN)
+    weight, keep, rate = carry_weights(retain)
     causal = jnp.arange(SEG_LEN)[:, None] >= jnp.arange(SEG_LEN)[None, :]
+    blocks = jnp.repeat(jnp.repeat(block_mask[0], BLOCK, axis=0), BLOCK, axis=1)
+    same = document_index[:, None] == document_index[None, :]
+    bias = jnp.where(causal & same & (blocks == 1), 0.0, -jnp.inf).astype(F32)
+    query, pairs = gather_project(n, 0, 0, tokens, attn_gain[:1], w_query, w_kv, tables)
     rest = tokens
-    query, pairs = gather_project(n, 0, 0, tokens, attn_gain[:1], w_query, w_kv, tables)
     stored = []
     for layer in range(DEPTH_NUMBER):
-        pairs = pairs.reshape(rows_all, local_kv, 2, HD)
-        lookup_vectors = pairs[:, :, 0]
-        values = pairs[:, :, 1]
-        query = query.reshape(seg_local, SEG_LEN, local_kv, group, HD)
-        lookup_vectors = lookup_vectors.reshape(seg_local, SEG_LEN, local_kv, HD)
-        values = values.reshape(seg_local, SEG_LEN, local_kv, HD)
-        slots = slot_keys[layer].reshape(MEM, local_kv, group, HD)
-        write_scores = (
-            jnp.einsum(
-                "mkgd,sjkd->skgmj", slots, lookup_vectors, preferred_element_type=jnp.float32
-            )
-            * scale
+        attended, after = attend(
+            count, 5 + layer, query, pairs, slot_keys[layer], bias, mem_init[layer],
+            weight[layer], keep[layer], rate[layer],
         )
-        write_probs = jax.nn.softmax(write_scores, axis=-1).astype(jnp.bfloat16)
-        written = jnp.einsum(
-            "skgmj,sjkd->smkgd", write_probs, values, preferred_element_type=jnp.float32
-        ).reshape(seg_local, MEM, cols_query)
-        rates = jnp.repeat(retain[layer], HD, axis=1)[:, None, :]
-        keep_total = jnp.ones((1, cols_query), jnp.float32)
-        add_total = jnp.zeros((MEM, cols_query), jnp.float32)
-        segment = 0
-        keep_total = keep_total * rates[segment]
-        add_total = rates[segment] * add_total + (1.0 - rates[segment]) * written[segment]
-        identity = (
-            jnp.ones((1, cols_query), jnp.float32),
-            jnp.zeros((MEM, cols_query), jnp.float32),
-        )
-        keep_before, add_before = prefix((keep_total, add_total), "seg", combine, identity)
-        state = keep_before * mem_init[layer] + add_before
-        segment = 0
-        memory_read = state.astype(jnp.bfloat16).reshape(MEM, local_kv, group, HD)
-        state = rates[segment] * state + (1.0 - rates[segment]) * written[segment]
-        after_list = [state]
-        blocks = jnp.repeat(jnp.repeat(block_mask[segment], BLOCK, axis=0), BLOCK, axis=1)
-        allowed = causal & (docs[segment][:, None] == docs[segment][None, :]) & (blocks == 1)
-        slot_scores = (
-            jnp.einsum("ikgd,mkgd->kgim", query[segment], slots, preferred_element_type=jnp.float32)
-            * scale
-        )
-        token_scores = (
-            jnp.einsum(
-                "ikgd,jkd->kgij",
-                query[segment],
-                lookup_vectors[segment],
-                preferred_element_type=jnp.float32,
-            )
-            * scale
-        )
-        token_scores = jnp.where(allowed, token_scores, -jnp.inf)
-        probs = jax.nn.softmax(
-            jnp.concatenate([slot_scores, token_scores], axis=-1), axis=-1
-        ).astype(jnp.bfloat16)
-        result = jnp.einsum(
-            "kgim,mkgd->ikgd", probs[..., :MEM], memory_read, preferred_element_type=jnp.float32
-        )
-        result = result + jnp.einsum(
-            "kgij,jkd->ikgd", probs[..., MEM:], values[segment], preferred_element_type=jnp.float32
-        )
-        outputs = result.reshape(SEG_LEN, cols_query).astype(jnp.bfloat16)
-        stored.append(jnp.stack(after_list))
+        stored.append(after)
         widening = jnp.swapaxes(w_gate_up[layer], 0, 1)
         inner, rest = exchange(
-            n, layer, 1 + 2 * layer, outputs, w_out, rest, mlp_gain[layer : layer + 1], (widening,)
+            n, layer, 1 + 2 * layer, attended, w_out, rest, mlp_gain[layer : layer + 1], (widening,)
         )
         if layer + 1 < DEPTH_NUMBER:
             query, pairs, rest = exchange(
@@ -632,7 +730,7 @@
             )
         else:
             stream = scatter(n, layer, 2 + 2 * layer, inner, w_down, rest)
-    return (stream, jnp.stack(stored))
+    return (stream, jnp.stack(stored)[:, None])
 
 
 def solution(mesh):

time: 1070 us -> 396 us (0.37)
  Pallas kernels: 913 us -> 332 us
  other arithmetic: 48 us -> 1.3 us
  matrix products: 19.1 us -> 0 us
  between operations: 15.1 us -> 0.95 us
  blocking collectives: 20.2 us -> 9.16 us
    pallas_call x3, Pallas kernels: 815 us -> 201 us  [exchange(): pl.pallas_call(functools.partial(exchange_kernel, n, layer, wide), out_sh...]
    pallas_call x0 -> x2, Pallas kernels: none -> 32.3 us  [attend(): pl.pallas_call(functools.partial(attend_kernel, count), out_shape=[jax.Sh...]
    select_n x32 -> x1, other arithmetic: 29.5 us -> 0.25 us  [body(): bias = jnp.where(causal & same & (blocks == 1), 0.0, -jnp.inf).astype(F32)]
    dot_general x12 -> x0, matrix products: 19.1 us -> none  [the longest x2 6.19 us: body(): jnp.einsum('kgij,jkd->ikgd', probs[..., MEM:], values[segment], preferred...]
    all_gather x2 -> x1, blocking collectives: 20.2 us -> 9.16 us  [carry_weights(): rates = lax.all_gather(retain[:, 0], 'seg')]
  transfers between devices with their start and end apart: 2 -> 0, of which waited for: 1 -> 0; matrix products, arithmetic and copies ran while one was open for 5% -> 0% of each run, Pallas kernels for 0% -> 0%
where the time goes in v2:
time: 396 us
  Pallas kernels  332 us (84%)
  local copies, waits for them, and re-layouts  51.8 us (13%)
  blocking collectives  9.16 us (2%)
    pallas_call x3, Pallas kernels, exchange(): pl.pallas_call(functools.partial(exchange_kernel, n, layer, wide), out_sh...  201 us
    pallas_call x1, Pallas kernels, scatter(): pl.pallas_call(functools.partial(scatter_kernel, n, layer), out_shape=jax...  62.2 us
    pallas_call x1, Pallas kernels, gather_project(): pl.pallas_call(functools.partial(gather_kernel, n, layer), out_shape=[jax...  36.5 us
    pallas_call x2, Pallas kernels, attend(): pl.pallas_call(functools.partial(attend_kernel, count), out_shape=[jax.Sh...  32.3 us
    unnamed x55, local copies, waits for them, and re-layouts  14.5 us
    slice x1, local copies, waits for them, and re-layouts, body(): widening = jnp.swapaxes(w_gate_up[layer], 0, 1)  14 us
    transpose x1, local copies, waits for them, and re-layouts, body(): widening = jnp.swapaxes(w_gate_up[layer], 0, 1)  11.8 us
    all_gather x1, blocking collectives, carry_weights(): rates = lax.all_gather(retain[:, 0], 'seg')  9.16 us

profile of v2, /device:TPU:16, one launch (start us, length us, event | category | flops | bytes accessed | tf_op | source)
XLA Modules:
  0.0 395.6 jit_solution(8996210156296443501)
XLA Ops:
  0.7 9.2 %all-gather = f32[16,1,8]{2,1,0:T(1,128)S(1)} all-gather(f32[2,1,8]{2,1,0:T(1,128)} %param.22), channel_id=2, replica_groups=mesh['seg'=8,'head'=4] {'seg'}, dimensions={0}, use_global_device_ids=true | all-gather | bytes 576 | tf_op jit(solution)/shard_map/all_gather | solution.py:681
  11.8 1.6 copy-done
  13.4 1.2 copy-done.1
  14.6 0.9 copy-done.4
  15.6 0.9 copy-done.6
  17.5 0.9 copy-done.10
  18.4 36.5 %gather_project.1 = (bf16[512,512]{1,0:T(8,128)(2,1)S(1)}, bf16[512,256]{1,0:T(8,128)(2,1)S(1)}) custom-call(f32[128,2048]{1,0:T(8,128)S(1)} %copy-done.1, f32[1,2048]{1,0:T(1,128)S(1)} %get-tuple-element.43.gain, bf16[2,2048,512]{2,1,0:T(8,128)(2,1)} %refs_4_.1, bf16[2,2048,256]{2,1,0:T(8,128)(2,1)S(1)} %copy-done, f32[512,128]{1,0:T(8,128)S(1)} %copy-done.4, ...), custom_call_target="tpu_custom_call" | custom-call | tf_op jit(solution)/shard_map/gather_project/pallas_call | solution.py:435
  55.0 1.6 broadcast_in_dim.92
  57.7 13.3 %attend.2 = (bf16[512,512]{1,0:T(8,128)(2,1)S(1)}, f32[128,512]{1,0:T(8,128)S(1)}) custom-call(bf16[512,512]{1,0:T(8,128)(2,1)S(1)} %get-tuple-element.15.query, bf16[512,256]{1,0:T(8,128)(2,1)S(1)} %get-tuple-element.16.pairs, bf16[128,512]{1,0:T(8,128)(2,1)S(1)} %get-tuple-element.39.slots, f32[512,512]{1,0:T(8,128)S(1)} %fusion.2.bias, ...), custom_call_target="tpu_custom_call" | custom-call | tf_op jit(solution)/shard_map/attend/pallas_call | solution.py:658
  71.0 14.0 %fusion.4 = (bf16[1,2048,2,1024]{3,2,1,0:T(2,128)(2,1)S(1)}, bf16[1,2048,2,1024]{3,2,1,0:T(2,128)(2,1)}) fusion(bf16[2,2048,2,1024]{3,2,1,0:T(2,128)(2,1)} %param.28), kind=kLoop, calls=%fused_computation.22 | loop fusion | bytes 33554432 | tf_op jit(solution)/shard_map/slice | solution.py:722
  85.1 11.8 %copy_bitcast_fusion = (bf16[2,2048,1024]{2,1,0:T(8,128)(2,1)}, bf16[2,2048,1024]{2,1,0:T(8,128)(2,1)}) fusion(bf16[1,2048,2,1024]{3,2,1,0:T(2,128)(2,1)S(1)} %get-tuple-element.34, bf16[1,2048,2,1024]{3,2,1,0:T(2,128)(2,1)} %get-tuple-element.35), kind=kLoop, calls=%fused_computation | loop fusion | bytes 33554432 | tf_op jit(solution)/shard_map/transpose | solution.py:722
  97.6 66.2 %exchange.3 = (bf16[512,1024]{1,0:T(8,128)(2,1)S(1)}, f32[256,2048]{1,0:T(8,128)S(1)}) custom-call(bf16[512,512]{1,0:T(8,128)(2,1)S(1)} %get-tuple-element.17.refs_0_, bf16[2,512,2048]{2,1,0:T(8,128)(2,1)} %refs_1_.5, f32[128,2048]{1,0:T(8,128)S(1)} %copy-done.2, f32[1,2048]{1,0:T(1,128)S(1)} %get-tuple-element.41.refs_3_, ...), custom_call_target="tpu_custom_call" | custom-call | tf_op jit(solution)/shard_map/exchange/pallas_call | solution.py:466
  163.7 1.4 copy-done.3
  165.1 68.3 %exchange.4 = (bf16[512,512]{1,0:T(8,128)(2,1)S(1)}, bf16[512,256]{1,0:T(8,128)(2,1)S(1)}, f32[256,2048]{1,0:T(8,128)S(1)}) custom-call(bf16[512,1024]{1,0:T(8,128)(2,1)S(1)} %get-tuple-element.18.refs_0_, bf16[2,1024,2048]{2,1,0:T(8,128)(2,1)} %w_hbm.1, f32[256,2048]{1,0:T(8,128)} %copy-done.3, f32[1,2048]{1,0:T(1,128)S(1)} %get-tuple-element.42.refs_3_, ...), custom_call_target="tpu_custom_call" | custom-call | tf_op jit(solution)/shard_map/exchange/pallas_call | solution.py:466
  236.5 1.3 broadcast_in_dim.108
  237.8 1.3 broadcast_in_dim.109.keep
  239.1 1.3 broadcast_in_dim.110
  240.4 1.3 broadcast_in_dim.111.rate
  241.7 1.0 copy-done.13
  242.7 0.9 copy-done.15
  245.0 19.0 %attend.3 = (bf16[512,512]{1,0:T(8,128)(2,1)S(1)}, f32[128,512]{1,0:T(8,128)S(1)}) custom-call(bf16[512,512]{1,0:T(8,128)(2,1)S(1)} %copy-done.13, bf16[512,256]{1,0:T(8,128)(2,1)S(1)} %copy-done.15, bf16[128,512]{1,0:T(8,128)(2,1)S(1)} %get-tuple-element.38.slots, f32[512,512]{1,0:T(8,128)S(1)} %fusion.2.bias, f32[128,512]{1,0:T(8,128)S(1)} %get-tuple-element.36.initial, ...), custom_call_target="tpu_custom_call" | custom-call | tf_op jit(solution)/shard_map/attend/pallas_call | solution.py:658
  264.7 66.9 %exchange.5 = (bf16[512,1024]{1,0:T(8,128)(2,1)S(1)}, f32[256,2048]{1,0:T(8,128)S(1)}) custom-call(bf16[512,512]{1,0:T(8,128)(2,1)S(1)} %get-tuple-element.22.refs_0_, bf16[2,512,2048]{2,1,0:T(8,128)(2,1)} %refs_1_.5, f32[256,2048]{1,0:T(8,128)S(1)} %get-tuple-element.23.refs_2_, f32[1,2048]{1,0:T(1,128)S(1)} %copy-done.18, ...), custom_call_target="tpu_custom_call" | custom-call | tf_op jit(solution)/shard_map/exchange/pallas_call | solution.py:466
  331.6 62.2 %scatter.1 = f32[128,2048]{1,0:T(8,128)S(1)} custom-call(bf16[512,1024]{1,0:T(8,128)(2,1)S(1)} %get-tuple-element.24.x, bf16[2,1024,2048]{2,1,0:T(8,128)(2,1)} %w_hbm.1, f32[256,2048]{1,0:T(8,128)S(1)} %get-tuple-element.25.rest), custom_call_target="tpu_custom_call" | custom-call | tf_op jit(solution)/shard_map/scatter/pallas_call | solution.py:491
  394.6 1.0 copy.37
  (70 shorter events, 10.4 us)
Async XLA Ops:
  0.6 56.3 %copy-start.25 = (f32[2,1,8]{2,1,0:T(1,128)S(1)}, f32[2,1,8]{2,1,0:T(1,128)}, u32[]{:S(2)}) copy-start(f32[2,1,8]{2,1,0:T(1,128)} %param.22) | copy-start | bytes 196
  0.6 54.3 %copy-start.26 = (s32[1,4,4]{2,1,0:T(4,128)S(1)}, s32[1,4,4]{2,1,0:T(4,128)}, u32[]{:S(2)}) copy-start(s32[1,4,4]{2,1,0:T(4,128)} %param.19) | copy-start | bytes 196
  0.7 56.0 %copy-start.24 = (s32[512]{0:T(512)S(1)}, s32[512]{0:T(512)}, u32[]{:S(2)}) copy-start(s32[512]{0:T(512)} %param.18) | copy-start | bytes 6148
  11.8 1.6 copy-start
  13.4 1.2 copy-start.1
  14.6 0.9 copy-start.4
  15.6 0.9 copy-start.6
  16.5 0.9 copy-start.8
  17.5 0.9 copy-start.10
  18.4 38.5 %copy-start.21 = (f32[2,128,512]{2,1,0:T(8,128)S(1)}, f32[2,128,512]{2,1,0:T(8,128)}, u32[]{:S(2)}) copy-start(f32[2,128,512]{2,1,0:T(8,128)} %param.21) | copy-start | bytes 1572868
  18.4 38.5 %copy-start.22 = (bf16[2,128,512]{2,1,0:T(8,128)(2,1)S(1)}, bf16[2,128,512]{2,1,0:T(8,128)(2,1)}, u32[]{:S(2)}) copy-start(bf16[2,128,512]{2,1,0:T(8,128)(2,1)} %param.20) | copy-start | bytes 786436
  71.0 14.1 %copy-start.16 = (f32[128,512]{1,0:T(8,128)}, f32[128,512]{1,0:T(8,128)S(1)}, u32[]{:S(2)}) copy-start(f32[128,512]{1,0:T(8,128)S(1)} %get-tuple-element.26) | copy-start | bytes 786436
  85.0 11.9 %copy-start.23 = (f32[2,2048]{1,0:T(2,128)S(1)}, f32[2,2048]{1,0:T(2,128)}, u32[]{:S(2)}) copy-start(f32[2,2048]{1,0:T(2,128)} %param.24) | copy-start | bytes 49156
  85.0 12.5 %copy-start.2 = (f32[128,2048]{1,0:T(8,128)S(1)}, f32[128,2048]{1,0:T(8,128)}, u32[]{:S(2)}) copy-start(f32[128,2048]{1,0:T(8,128)} %refs_2_.1) | copy-start | bytes 3145732
  96.9 68.2 %copy-start.5 = (f32[512,128]{1,0:T(8,128)S(1)}, f32[512,128]{1,0:T(8,128)}, u32[]{:S(2)}) copy-start(f32[512,128]{1,0:T(8,128)} %constant.23.clone.cos_q.refs_6_) | copy-start | bytes 786436
  96.9 68.2 %copy-start.7 = (f32[512,128]{1,0:T(8,128)S(1)}, f32[512,128]{1,0:T(8,128)}, u32[]{:S(2)}) copy-start(f32[512,128]{1,0:T(8,128)} %constant.24.clone.sin_q.refs_7_) | copy-start | bytes 786436
  96.9 68.2 %copy-start.9 = (f32[512,128]{1,0:T(8,128)S(1)}, f32[512,128]{1,0:T(8,128)}, u32[]{:S(2)}) copy-start(f32[512,128]{1,0:T(8,128)} %constant.25.clone.cos_kv.refs_8_) | copy-start | bytes 786436
  96.9 68.2 %copy-start.11 = (f32[512,128]{1,0:T(8,128)S(1)}, f32[512,128]{1,0:T(8,128)}, u32[]{:S(2)}) copy-start(f32[512,128]{1,0:T(8,128)} %constant.26.clone.sin_kv.refs_9_) | copy-start | bytes 786436
  163.7 1.4 copy-start.3
  233.5 0.8 copy-start.12
  234.3 0.7 copy-start.14
  241.7 1.0 copy-start.13
  242.7 0.9 copy-start.15
  331.6 62.2 %copy-start.17 = (f32[128,512]{1,0:T(8,128)S(1)}, f32[128,512]{1,0:T(8,128)}, u32[]{:S(2)}) copy-start(f32[128,512]{1,0:T(8,128)} %copy-done.16) | copy-start | bytes 786436
  (3 other events, 2.0 us)

commit v3 on v2

--- a/solution.py
+++ b/solution.py
@@ -15,7 +15,8 @@
 SEG_LEN = 512
 BLOCK = 128
 DEPTH_NUMBER = 2
-CHUNK = 32
+CHUNK = 16
+PIECE = 32
 LAG = 2
 MESH = pl.DeviceIdType.MESH
 F32 = jnp.float32
@@ -129,19 +130,19 @@
     for copy in loads:
         copy.start()
     mine = tokens.shape[0]
-    pieces = mine // CHUNK
+    pieces = mine // PIECE
     enter(me, n)
 
     def hop(way, shard, piece):
-        rows = pl.ds(pl.multiple_of(shard * mine + piece * CHUNK, CHUNK), CHUNK)
+        rows = pl.ds(pl.multiple_of(shard * mine + piece * PIECE, PIECE), PIECE)
         to = me + 1 if way == 0 else me - 1
         to = jnp.clip(to, 0, n - 1)
         at = shard * pieces + piece
         return remote(x.at[rows], x.at[rows], send.at[way, at], recv.at[way, at], to)
 
     for piece in range(pieces):
-        rows = pl.ds(pl.multiple_of(me * mine + piece * CHUNK, CHUNK), CHUNK)
-        x[rows, :] = normed_rows(tokens[piece * CHUNK : (piece + 1) * CHUNK, :], gain[...])
+        rows = pl.ds(pl.multiple_of(me * mine + piece * PIECE, PIECE), PIECE)
+        x[rows, :] = normed_rows(tokens[piece * PIECE : (piece + 1) * PIECE, :], gain[...])
 
         @pl.when(me < n - 1)
         def _():
@@ -224,10 +225,8 @@
     count = half // CHUNK
     enter(me, n)
     loads[0].wait()
-    for block in range(0, half, BLOCK):
-        for way in (0, 1):
-            partial_rows(pl.ds(way * half + block, BLOCK), x, w, part)
-    add_rest(me, n, part, rest)
+    for way in (0, 1):
+        partial_rows(pl.ds(way * half, BLOCK), x, w, part)
 
     def place(way, t):
         return pl.ds(pl.multiple_of(way * half + t * CHUNK, CHUNK), CHUNK)
@@ -295,6 +294,13 @@
             far = n - 1 - me if way == 0 else me
             down.append(now - LAG * far)
             back.append(now - LAG * (n - 1) - LAG * (n - 1 - far))
+        @pl.when(now == LAG)
+        def _():
+            for way in (0, 1):
+                for block in range(BLOCK, half, BLOCK):
+                    partial_rows(pl.ds(way * half + block, BLOCK), x, w, part)
+            add_rest(me, n, part, rest)
+
         for way in (0, 1):
 
             @pl.when((down[way] >= 0) & (down[way] < count))
@@ -360,12 +366,17 @@
         return remote(outgoing.at[way, rows], arriving.at[way, rows], send.at[way, at],
                       recv.at[way, at], to)
 
-    def step(i, carry):
+    hops = (n - 1) * pieces
+
+    def step(now, carry):
         for way in (0, 1):
+            i = now - LAG * (me if way == 0 else n - 1 - me)
+            valid = (i >= 0) & (i < hops)
+            i = jnp.clip(i, 0, hops - 1)
             shard = n - 1 - i // pieces if way == 0 else i // pieces
             at = shard * pieces + i % pieces
             rows = place(at)
-            ahead = me < shard if way == 0 else me > shard
+            ahead = valid & ((me < shard) if way == 0 else (me > shard))
             edge = me == 0 if way == 0 else me == n - 1
 
             @pl.when(ahead & edge)
@@ -383,7 +394,7 @@
 
         return carry
 
-    lax.fori_loop(0, (n - 1) * pieces, step, 0)
+    lax.fori_loop(0, hops + LAG * (n - 1), step, 0)
     for piece in range(pieces):
         at = me * pieces + piece
         here = slice(piece * CHUNK, (piece + 1) * CHUNK)
@@ -442,8 +453,8 @@
             pltpu.VMEM(wq.shape[1:], BF16),
             pltpu.VMEM(wkv.shape[1:], BF16),
             dma(2),
-            dma(2, rows // CHUNK),
-            dma(2, rows // CHUNK),
+            dma(2, rows // PIECE),
+            dma(2, rows // PIECE),
         ],
         compiler_params=parameters(number),
         name="gather_project",

time: 396 us -> 377 us (0.952); the launches traced: 396 us -> 371 us
  Pallas kernels: 332 us -> 308 us
    pallas_call x1, Pallas kernels: 62.2 us -> 42.2 us  [scatter(): pl.pallas_call(functools.partial(scatter_kernel, n, layer), out_shape=jax...]
where the time goes in v3:
time: 377 us; the launch traced here: 371 us
  Pallas kernels  308 us (82%)
  local copies, waits for them, and re-layouts  51.8 us (14%)
  blocking collectives  9.16 us (2%)
    pallas_call x3, Pallas kernels, exchange(): pl.pallas_call(functools.partial(exchange_kernel, n, layer, wide), out_sh...  198 us
    pallas_call x1, Pallas kernels, scatter(): pl.pallas_call(functools.partial(scatter_kernel, n, layer), out_shape=jax...  42.2 us
    pallas_call x1, Pallas kernels, gather_project(): pl.pallas_call(functools.partial(gather_kernel, n, layer), out_shape=[jax...  36.5 us
    pallas_call x2, Pallas kernels, attend(): pl.pallas_call(functools.partial(attend_kernel, count), out_shape=[jax.Sh...  31.2 us
    unnamed x55, local copies, waits for them, and re-layouts  14.5 us
    slice x1, local copies, waits for them, and re-layouts, body(): widening = jnp.swapaxes(w_gate_up[layer], 0, 1)  14 us
    transpose x1, local copies, waits for them, and re-layouts, body(): widening = jnp.swapaxes(w_gate_up[layer], 0, 1)  11.8 us
    all_gather x1, blocking collectives, carry_weights(): rates = lax.all_gather(retain[:, 0], 'seg')  9.16 us

profile of v3, /device:TPU:16, one launch (start us, length us, event | category | flops | bytes accessed | tf_op | source)
XLA Modules:
  0.0 371.2 jit_solution(10326516597522261848)
XLA Ops:
  0.7 9.2 %all-gather = f32[16,1,8]{2,1,0:T(1,128)S(1)} all-gather(f32[2,1,8]{2,1,0:T(1,128)} %param.22), channel_id=2, replica_groups=mesh['seg'=8,'head'=4] {'seg'}, dimensions={0}, use_global_device_ids=true | all-gather | bytes 576 | tf_op jit(solution)/shard_map/all_gather | solution.py:692
  11.8 1.6 copy-done
  13.4 1.2 copy-done.1
  14.6 0.9 copy-done.4
  16.5 0.9 copy-done.8
  17.5 0.9 copy-done.10
  18.4 36.5 %gather_project.1 = (bf16[512,512]{1,0:T(8,128)(2,1)S(1)}, bf16[512,256]{1,0:T(8,128)(2,1)S(1)}) custom-call(f32[128,2048]{1,0:T(8,128)S(1)} %copy-done.1, f32[1,2048]{1,0:T(1,128)S(1)} %get-tuple-element.43.gain, bf16[2,2048,512]{2,1,0:T(8,128)(2,1)} %refs_4_.1, bf16[2,2048,256]{2,1,0:T(8,128)(2,1)S(1)} %copy-done, f32[512,128]{1,0:T(8,128)S(1)} %copy-done.4, ...), custom_call_target="tpu_custom_call" | custom-call | tf_op jit(solution)/shard_map/gather_project/pallas_call | solution.py:446
  55.0 1.6 broadcast_in_dim.92
  57.7 13.3 %attend.2 = (bf16[512,512]{1,0:T(8,128)(2,1)S(1)}, f32[128,512]{1,0:T(8,128)S(1)}) custom-call(bf16[512,512]{1,0:T(8,128)(2,1)S(1)} %get-tuple-element.15.query, bf16[512,256]{1,0:T(8,128)(2,1)S(1)} %get-tuple-element.16.pairs, bf16[128,512]{1,0:T(8,128)(2,1)S(1)} %get-tuple-element.39.slots, f32[512,512]{1,0:T(8,128)S(1)} %fusion.2.bias, ...), custom_call_target="tpu_custom_call" | custom-call | tf_op jit(solution)/shard_map/attend/pallas_call | solution.py:669
  71.0 14.0 %fusion.4 = (bf16[1,2048,2,1024]{3,2,1,0:T(2,128)(2,1)S(1)}, bf16[1,2048,2,1024]{3,2,1,0:T(2,128)(2,1)}) fusion(bf16[2,2048,2,1024]{3,2,1,0:T(2,128)(2,1)} %param.28), kind=kLoop, calls=%fused_computation.22 | loop fusion | bytes 33554432 | tf_op jit(solution)/shard_map/slice | solution.py:733
  85.1 11.8 %copy_bitcast_fusion = (bf16[2,2048,1024]{2,1,0:T(8,128)(2,1)}, bf16[2,2048,1024]{2,1,0:T(8,128)(2,1)}) fusion(bf16[1,2048,2,1024]{3,2,1,0:T(2,128)(2,1)S(1)} %get-tuple-element.34, bf16[1,2048,2,1024]{3,2,1,0:T(2,128)(2,1)} %get-tuple-element.35), kind=kLoop, calls=%fused_computation | loop fusion | bytes 33554432 | tf_op jit(solution)/shard_map/transpose | solution.py:733
  97.6 65.3 %exchange.3 = (bf16[512,1024]{1,0:T(8,128)(2,1)S(1)}, f32[256,2048]{1,0:T(8,128)S(1)}) custom-call(bf16[512,512]{1,0:T(8,128)(2,1)S(1)} %get-tuple-element.17.refs_0_, bf16[2,512,2048]{2,1,0:T(8,128)(2,1)} %refs_1_.5, f32[128,2048]{1,0:T(8,128)S(1)} %copy-done.2, f32[1,2048]{1,0:T(1,128)S(1)} %get-tuple-element.41.refs_3_, ...), custom_call_target="tpu_custom_call" | custom-call | tf_op jit(solution)/shard_map/exchange/pallas_call | solution.py:477
  162.9 1.4 copy-done.3
  164.3 66.4 %exchange.4 = (bf16[512,512]{1,0:T(8,128)(2,1)S(1)}, bf16[512,256]{1,0:T(8,128)(2,1)S(1)}, f32[256,2048]{1,0:T(8,128)S(1)}) custom-call(bf16[512,1024]{1,0:T(8,128)(2,1)S(1)} %get-tuple-element.18.refs_0_, bf16[2,1024,2048]{2,1,0:T(8,128)(2,1)} %w_hbm.1, f32[256,2048]{1,0:T(8,128)} %copy-done.3, f32[1,2048]{1,0:T(1,128)S(1)} %get-tuple-element.42.refs_3_, ...), custom_call_target="tpu_custom_call" | custom-call | tf_op jit(solution)/shard_map/exchange/pallas_call | solution.py:477
  233.7 1.3 broadcast_in_dim.108
  235.1 1.3 broadcast_in_dim.109.keep
  236.4 1.3 broadcast_in_dim.110
  237.7 1.3 broadcast_in_dim.111.rate
  239.0 1.0 copy-done.13
  240.0 0.9 copy-done.15
  242.2 18.0 %attend.3 = (bf16[512,512]{1,0:T(8,128)(2,1)S(1)}, f32[128,512]{1,0:T(8,128)S(1)}) custom-call(bf16[512,512]{1,0:T(8,128)(2,1)S(1)} %copy-done.13, bf16[512,256]{1,0:T(8,128)(2,1)S(1)} %copy-done.15, bf16[128,512]{1,0:T(8,128)(2,1)S(1)} %get-tuple-element.38.slots, f32[512,512]{1,0:T(8,128)S(1)} %fusion.2.bias, f32[128,512]{1,0:T(8,128)S(1)} %get-tuple-element.36.initial, ...), custom_call_target="tpu_custom_call" | custom-call | tf_op jit(solution)/shard_map/attend/pallas_call | solution.py:669
  260.9 66.2 %exchange.5 = (bf16[512,1024]{1,0:T(8,128)(2,1)S(1)}, f32[256,2048]{1,0:T(8,128)S(1)}) custom-call(bf16[512,512]{1,0:T(8,128)(2,1)S(1)} %get-tuple-element.22.refs_0_, bf16[2,512,2048]{2,1,0:T(8,128)(2,1)} %refs_1_.5, f32[256,2048]{1,0:T(8,128)S(1)} %get-tuple-element.23.refs_2_, f32[1,2048]{1,0:T(1,128)S(1)} %copy-done.18, ...), custom_call_target="tpu_custom_call" | custom-call | tf_op jit(solution)/shard_map/exchange/pallas_call | solution.py:477
  327.1 42.2 %scatter.1 = f32[128,2048]{1,0:T(8,128)S(1)} custom-call(bf16[512,1024]{1,0:T(8,128)(2,1)S(1)} %get-tuple-element.24.x, bf16[2,1024,2048]{2,1,0:T(8,128)(2,1)} %w_hbm.1, f32[256,2048]{1,0:T(8,128)S(1)} %get-tuple-element.25.rest), custom_call_target="tpu_custom_call" | custom-call | tf_op jit(solution)/shard_map/scatter/pallas_call | solution.py:502
  370.2 1.0 copy.37
  (70 shorter events, 10.4 us)
Async XLA Ops:
  0.6 56.3 %copy-start.25 = (f32[2,1,8]{2,1,0:T(1,128)S(1)}, f32[2,1,8]{2,1,0:T(1,128)}, u32[]{:S(2)}) copy-start(f32[2,1,8]{2,1,0:T(1,128)} %param.22) | copy-start | bytes 196
  0.6 54.3 %copy-start.26 = (s32[1,4,4]{2,1,0:T(4,128)S(1)}, s32[1,4,4]{2,1,0:T(4,128)}, u32[]{:S(2)}) copy-start(s32[1,4,4]{2,1,0:T(4,128)} %param.19) | copy-start | bytes 196
  0.7 56.0 %copy-start.24 = (s32[512]{0:T(512)S(1)}, s32[512]{0:T(512)}, u32[]{:S(2)}) copy-start(s32[512]{0:T(512)} %param.18) | copy-start | bytes 6148
  11.8 1.6 copy-start
  13.4 1.2 copy-start.1
  14.6 0.9 copy-start.4
  15.6 0.9 copy-start.6
  16.5 0.9 copy-start.8
  17.5 0.9 copy-start.10
  18.4 38.5 %copy-start.21 = (f32[2,128,512]{2,1,0:T(8,128)S(1)}, f32[2,128,512]{2,1,0:T(8,128)}, u32[]{:S(2)}) copy-start(f32[2,128,512]{2,1,0:T(8,128)} %param.21) | copy-start | bytes 1572868
  18.4 38.5 %copy-start.22 = (bf16[2,128,512]{2,1,0:T(8,128)(2,1)S(1)}, bf16[2,128,512]{2,1,0:T(8,128)(2,1)}, u32[]{:S(2)}) copy-start(bf16[2,128,512]{2,1,0:T(8,128)(2,1)} %param.20) | copy-start | bytes 786436
  71.0 14.1 %copy-start.16 = (f32[128,512]{1,0:T(8,128)}, f32[128,512]{1,0:T(8,128)S(1)}, u32[]{:S(2)}) copy-start(f32[128,512]{1,0:T(8,128)S(1)} %get-tuple-element.26) | copy-start | bytes 786436
  85.0 11.9 %copy-start.23 = (f32[2,2048]{1,0:T(2,128)S(1)}, f32[2,2048]{1,0:T(2,128)}, u32[]{:S(2)}) copy-start(f32[2,2048]{1,0:T(2,128)} %param.24) | copy-start | bytes 49156
  85.0 12.5 %copy-start.2 = (f32[128,2048]{1,0:T(8,128)S(1)}, f32[128,2048]{1,0:T(8,128)}, u32[]{:S(2)}) copy-start(f32[128,2048]{1,0:T(8,128)} %refs_2_.1) | copy-start | bytes 3145732
  96.9 67.4 %copy-start.5 = (f32[512,128]{1,0:T(8,128)S(1)}, f32[512,128]{1,0:T(8,128)}, u32[]{:S(2)}) copy-start(f32[512,128]{1,0:T(8,128)} %constant.23.clone.cos_q.refs_6_) | copy-start | bytes 786436
  96.9 67.4 %copy-start.7 = (f32[512,128]{1,0:T(8,128)S(1)}, f32[512,128]{1,0:T(8,128)}, u32[]{:S(2)}) copy-start(f32[512,128]{1,0:T(8,128)} %constant.24.clone.sin_q.refs_7_) | copy-start | bytes 786436
  96.9 67.4 %copy-start.9 = (f32[512,128]{1,0:T(8,128)S(1)}, f32[512,128]{1,0:T(8,128)}, u32[]{:S(2)}) copy-start(f32[512,128]{1,0:T(8,128)} %constant.25.clone.cos_kv.refs_8_) | copy-start | bytes 786436
  96.9 67.4 %copy-start.11 = (f32[512,128]{1,0:T(8,128)S(1)}, f32[512,128]{1,0:T(8,128)}, u32[]{:S(2)}) copy-start(f32[512,128]{1,0:T(8,128)} %constant.26.clone.sin_kv.refs_9_) | copy-start | bytes 786436
  162.9 1.4 copy-start.3
  230.7 0.8 copy-start.12
  231.5 0.7 copy-start.14
  239.0 1.0 copy-start.13
  240.0 0.9 copy-start.15
  327.1 42.3 %copy-start.17 = (f32[128,512]{1,0:T(8,128)S(1)}, f32[128,512]{1,0:T(8,128)}, u32[]{:S(2)}) copy-start(f32[128,512]{1,0:T(8,128)} %copy-done.16) | copy-start | bytes 786436
  (3 other events, 2.0 us)
